TPU v7x, 128 devices: a whole 4x4x4 slice. The times are simulated.
128 devices in a mesh: seq: 8 (over z, core), tp: 16 (over x, y).
Axes of the slice: x: 4, y: 4, z: 4, core: 2. Of those that a mesh axis runs over, the one named last changes fastest.
Arguments:
- hidden_in: bfloat16 [2048, 6144], P('seq', 'tp'), may hold values from -6 to 6
- norm_gain: bfloat16 [6144], replicated, may hold values from 0.099609375 to 1.8984375
- w_query: bfloat16 [6144, 6144], P(None, 'tp'), may hold values from -0.078125 to 0.078125
- w_keyval: bfloat16 [6144, 2048], P(None, 'tp'), may hold values from -0.15625 to 0.15625
- w_out: bfloat16 [6144, 6144], P('tp'), may hold values from -0.5 to 0.5
- key_pool: bfloat16 [1024, 128, 1024], P(('seq', 'tp')), may hold values from -512 to 512
- value_pool: bfloat16 [1024, 128, 1024], P(('seq', 'tp')), may hold values from -6 to 6
- block_table: int32 [32, 64], replicated, may hold values from -1 to 1023, as said below
- prefix_lengths: int32 [32], replicated, may hold values from 1 to 8192, as said below
- row_request: int32 [2048], P('seq'), may hold values from 0 to 31, as said below
Outputs:
- attention_out: bfloat16 [2048, 6144], P(('seq', 'tp'))
Inputs may be any that keep to these rules, and one draw needn't show every extreme that they name: `block_table`: row r lists its request's pool blocks: the first ceil(prefix_lengths[r] / 128) entries are distinct block ids b with b % 8 equal to r // 4, the rest are -1; no block is listed by two requests; the blocks listed by one group hold at most 128 blocks. `prefix_lengths`: in every group one request has exactly 8192 tokens. `row_request`: row i names a request of group i // 256, that is a request r with r // 4 == i // 256.
All inputs are finite; a program needn't handle non-finite values.
Results may differ from a plain program's by a relative error of at most 0.02.
The roundings to bfloat16 on the way count: a program that leaves them out, or rounds other values in their place, can miss the bound.
Values may be sent and summed in bfloat16 or wider, within the bound.
A program may use at most 128 MiB of HBM per device.

v0:
```python
import jax
import jax.numpy as jnp
from jax import lax
from jax.sharding import PartitionSpec as P

HD = 128
BLK = 128
REQ_GRP = 4


EPSILON = 1e-05


def partner_2(value, axis, stride):
    mask = 2**stride
    pairs = [(source, source ^ mask) for source in range(lax.axis_size(axis))]
    return lax.ppermute(value, axis, pairs)


def per_device(
    hidden_in,
    norm_gain,
    w_query,
    w_keyval,
    w_out,
    key_pool,
    value_pool,
    block_table,
    prefix_lengths,
    row_request,
):
    seq_count = lax.axis_size("seq")
    tp_count = lax.axis_size("tp")
    group_index = lax.axis_index("seq")
    tp_rank = lax.axis_index("tp")
    row_count = hidden_in.shape[0]
    full_rows = lax.all_gather(hidden_in, "tp", axis=1, tiled=True)
    widened = full_rows.astype(jnp.float32)
    normed = (
        widened
        * lax.rsqrt(jnp.mean(widened * widened, axis=1, keepdims=True) + EPSILON)
        * norm_gain.astype(jnp.float32)
    ).astype(jnp.bfloat16)
    heads_dev = w_query.shape[1] // HD
    queries = (
        jnp.dot(normed, w_query, preferred_element_type=jnp.float32)
        .astype(jnp.bfloat16)
        .reshape(row_count, heads_dev, HD)
    )
    pieces = jnp.dot(normed, w_keyval, preferred_element_type=jnp.float32).astype(jnp.bfloat16)
    partner = partner_2(pieces, "tp", 0)
    is_even = tp_rank % 2 == 0
    key_new = jnp.where(is_even, pieces, partner)
    value_new = jnp.where(is_even, partner, pieces)
    blocks_dev = key_pool.shape[0]
    per_group = blocks_dev // seq_count
    kv_heads = key_pool.shape[2] // HD
    copy_count = tp_count // kv_heads

    def arrange(pool_part):
        shaped = pool_part.reshape(per_group, seq_count, BLK, kv_heads, HD)
        shaped = jnp.repeat(shaped, copy_count, axis=3)
        shaped = jnp.transpose(shaped, (1, 3, 0, 2, 4))
        return shaped

    key_send = arrange(key_pool)
    value_send = arrange(value_pool)
    total_pieces = seq_count * tp_count * per_group
    key_local, value_local = (
        lax.all_to_all(
            key_send.reshape(total_pieces, BLK, HD),
            ("seq", "tp"),
            split_axis=0,
            concat_axis=0,
            tiled=True,
        ),
        lax.all_to_all(
            value_send.reshape(total_pieces, BLK, HD),
            ("seq", "tp"),
            split_axis=0,
            concat_axis=0,
            tiled=True,
        ),
    )
    key_tokens = key_local.reshape(-1, HD)
    value_tokens = value_local.reshape(-1, HD)
    total_tokens = key_tokens.shape[0]
    total_blocks = total_tokens // BLK
    group_table = lax.dynamic_slice_in_dim(block_table, group_index * REQ_GRP, REQ_GRP, 0)
    lengths_group = lax.dynamic_slice_in_dim(prefix_lengths, group_index * REQ_GRP, REQ_GRP, 0)
    max_blocks = block_table.shape[1]
    req_ids = group_index * REQ_GRP + jnp.arange(REQ_GRP, dtype=jnp.int32)
    listed = group_table >= 0
    local_ids = jnp.where(listed, group_table // seq_count, total_blocks)
    owner_src = jnp.broadcast_to(req_ids[:, None], (REQ_GRP, max_blocks))
    pos_src = jnp.broadcast_to(
        jnp.arange(max_blocks, dtype=jnp.int32)[None, :], (REQ_GRP, max_blocks)
    )
    block_owner = (
        jnp.full((total_blocks,), -1, jnp.int32)
        .at[local_ids.reshape(-1)]
        .set(owner_src.reshape(-1), mode="drop")
    )
    block_pos = (
        jnp.zeros((total_blocks,), jnp.int32)
        .at[local_ids.reshape(-1)]
        .set(pos_src.reshape(-1), mode="drop")
    )
    owner_tok = jnp.repeat(block_owner, BLK)
    pos_tok = (block_pos[:, None] * BLK + jnp.arange(BLK, dtype=jnp.int32)[None, :]).reshape(-1)
    matches = (row_request[:, None] == req_ids[None, :]).astype(jnp.int32)
    row_len = jnp.sum(matches * lengths_group[None, :], axis=1)
    score_scale = 1.0 / HD**0.5
    self_score = (
        jnp.einsum("rhd,rd->rh", queries, key_new, preferred_element_type=jnp.float32) * score_scale
    )
    key_block = min(2048, total_tokens)
    block_turns = total_tokens // key_block

    def attend_block(block_index, carry):
        run_max, run_sum, accumulated = carry
        first_token = block_index * key_block
        key_part = lax.dynamic_slice_in_dim(key_tokens, first_token, key_block, 0)
        value_part = lax.dynamic_slice_in_dim(value_tokens, first_token, key_block, 0)
        owner_part = lax.dynamic_slice_in_dim(owner_tok, first_token, key_block, 0)
        position_part = lax.dynamic_slice_in_dim(pos_tok, first_token, key_block, 0)
        allowed = (owner_part[None, :] == row_request[:, None]) & (
            position_part[None, :] < row_len[:, None]
        )
        scores = (
            jnp.einsum("rhd,td->rht", queries, key_part, preferred_element_type=jnp.float32)
            * score_scale
        )
        scores = jnp.where(allowed[:, None, :], scores, -1e30)
        new_max = jnp.maximum(run_max, jnp.max(scores, axis=2))
        weights = jnp.exp(scores - new_max[:, :, None])
        factor = jnp.exp(run_max - new_max)
        run_sum = run_sum * factor + jnp.sum(weights, axis=2)
        accumulated = accumulated * factor[:, :, None] + jnp.einsum(
            "rht,td->rhd",
            weights.astype(jnp.bfloat16),
            value_part,
            preferred_element_type=jnp.float32,
        )
        return (new_max, run_sum, accumulated)

    start_acc = jnp.broadcast_to(
        value_new.astype(jnp.float32)[:, None, :], (row_count, heads_dev, HD)
    )
    start_sum = jnp.ones((row_count, heads_dev), jnp.float32)
    run_max, run_sum, accumulated = lax.fori_loop(
        0, block_turns, attend_block, (self_score, start_sum, start_acc)
    )
    attended = (
        (accumulated / run_sum[:, :, None]).astype(jnp.bfloat16).reshape(row_count, heads_dev * HD)
    )
    partials = jnp.dot(attended, w_out, preferred_element_type=jnp.float32)
    result = lax.psum_scatter(partials.astype(jnp.bfloat16), "tp", scatter_dimension=0, tiled=True)
    return result


def solution(mesh):
    return jax.shard_map(
        per_device,
        mesh=mesh,
        in_specs=(
            P("seq", "tp"),
            P(),
            P(None, "tp"),
            P(None, "tp"),
            P("tp", None),
            P(("seq", "tp"), None, None),
            P(("seq", "tp"), None, None),
            P(),
            P(),
            P("seq"),
        ),
        out_specs=P(("seq", "tp"), None),
        check_vma=False,
    )
```

profile of v0, /device:TPU:0, one launch (start us, length us, event | category | flops | bytes accessed | tf_op | source)
XLA Modules:
  0.0 311.2 jit_solution(6307376056974520533)
XLA Ops:
  6.5 1.6 copy-done
  8.1 0.6 copy_bitcast_fusion.1
  8.7 3.0 broadcast_in_dim.109
  11.7 11.7 %all-to-all-start = ((bf16[128,128,128]{2,1,0:T(8,128)(2,1)}), bf16[128,128,128]{2,1,0:T(8,128)(2,1)}, u32[]{:S(2)}, u32[]{:S(2)}) async-start(bf16[128,128,128]{2,1,0:T(8,128)(2,1)} %bitcast.71), calls=%async_computation | async-start | bytes 8388608 | tf_op jit(solution)/shard_map/all_to_all | solution.py:70
  23.5 0.7 all-gather.2.cloned.1.call-update
  24.2 3.5 %copy_bitcast_fusion = bf16[8,128,8,128]{3,1,2,0:T(8,128)(2,1)} fusion(bf16[8,128,1024]{2,1,0:T(8,128)(2,1)} %param.18), kind=kLoop, calls=%fused_computation.29 | loop fusion | bytes 4194304 | tf_op jit(solution)/shard_map/reshape | solution.py:61
  27.6 50.0 %all-to-all-done = bf16[128,128,128]{2,1,0:T(8,128)(2,1)} async-done(((bf16[128,128,128]{2,1,0:T(8,128)(2,1)}), bf16[128,128,128]{2,1,0:T(8,128)(2,1)}, u32[]{:S(2)}, u32[]{:S(2)}) %all-to-all-start) | async-done | bytes 4194336 | tf_op jit(solution)/shard_map/all_to_all | solution.py:70
  77.6 5.1 %broadcast_in_dim.111 = bf16[8,128,8,2,128]{4,1,3,2,0:T(8,128)(2,1)} broadcast(bf16[8,128,8,128]{3,1,2,0:T(8,128)(2,1)} %copy_bitcast_fusion), dimensions={0,1,2,4} | broadcast | bytes 6291456 | tf_op jit(solution)/shard_map/broadcast_in_dim | solution.py:62
  82.7 6.0 %all-to-all-start.1 = ((bf16[128,128,128]{2,1,0:T(8,128)(2,1)}), bf16[128,128,128]{2,1,0:T(8,128)(2,1)}, u32[]{:S(2)}, u32[]{:S(2)}) async-start(bf16[128,128,128]{2,1,0:T(8,128)(2,1)} %bitcast.70), calls=%async_computation.1 | async-start | bytes 8388608 | tf_op jit(solution)/shard_map/all_to_all | solution.py:77
  88.8 0.1 broadcast_in_dim.105
  88.9 0.1 reshape.169
  88.9 0.1 dynamic_slice.35
  89.0 0.7 fusion.25
  89.7 0.1 reshape.154
  89.8 0.1 reshape.177
  89.9 1.4 scatter_custom_fusion.1
  91.3 1.4 scatter_custom_fusion
  92.7 0.1 select_reduce_fusion
  92.8 0.1 add_bitcast_fusion
  92.9 51.4 %all-gather.2.cloned.1.call-done = bf16[256,6144]{1,0:T(8,128)(2,1)} async-done(((bf16[256,384]{1,0:T(8,128)(2,1)}), bf16[256,6144]{1,0:T(8,128)(2,1)}) %all-gather.2.cloned.1.call-update) | async-done | bytes 3145744 | tf_op jit(solution)/shard_map/all_gather | solution.py:37
  144.3 2.6 fusion.19
  146.9 3.6 %convolution_convert_fusion.2 = bf16[256,128]{1,0:T(8,128)(2,1)S(1)} fusion(bf16[6144,128]{1,0:T(8,128)(2,1)} %param.15, bf16[256,6144]{1,0:T(8,128)(2,1)} %all-gather.2.cloned.1.call-done, f32[6144]{0:T(1024)S(1)} %convert_element_type.33, f32[256]{0:T(256)S(1)} %add_rsqrt_fusion), kind=kOutput, calls=%fused_computation.32 | convolution fusion | flops 408977408 | bytes 4809728 | tf_op jit(solution)/shard_map/dot_general | solution.py:50
  150.6 0.3 collective-permute-start
  150.8 4.2 %convolution_convert_fusion.1 = bf16[256,384]{1,0:T(8,128)(2,1)S(1)} fusion(bf16[6144,384]{1,0:T(8,128)(2,1)} %param.14, bf16[256,6144]{1,0:T(8,128)(2,1)S(1)} %copy-done.1, f32[6144]{0:T(1024)S(1)} %convert_element_type.33, f32[256]{0:T(256)S(1)} %add_rsqrt_fusion), kind=kOutput, calls=%fused_computation.31 | convolution fusion | flops 1214349312 | bytes 8086528 | tf_op jit(solution)/shard_map/dot_general | solution.py:46
  155.1 0.1 copy.34
  155.2 0.2 copy.25
  155.4 0.1 copy.35
  155.5 0.1 multiply_reduce_fusion
  155.7 65.5 %while.18 = (s32[]{:T(128)}, f32[256,3]{0,1:T(4,128)S(1)}, f32[256,3]{0,1:T(4,128)S(1)}, f32[256,3,128]{2,0,1:T(8,128)S(1)}, s32[16384]{0:T(1024)S(1)}, /*index=...) while((s32[]{:T(128)}, f32[256,3]{0,1:T(4,128)S(1)}, ...), condition=%wide.region_7.8_spmd.clone, body=%wide.region_4.7_spmd.clone.sunk | while | flops 824379648 | bytes 23103708 | solution.py:151
  155.7 1.4 compare_and_fusion.2
  157.2 2.3 fusion.48
  159.5 1.4 fusion.49
  160.9 2.9 fusion.51
  163.9 1.4 compare_and_fusion.2
  165.3 2.3 fusion.48
  167.7 1.4 fusion.49
  169.1 2.9 fusion.51
  172.1 1.4 compare_and_fusion.2
  173.5 2.3 fusion.48
  175.9 1.4 fusion.49
  177.3 2.9 fusion.51
  180.3 1.4 compare_and_fusion.2
  181.7 2.3 fusion.48
  184.0 1.4 fusion.49
  185.4 2.9 fusion.51
  188.5 1.4 compare_and_fusion.2
  189.9 2.3 fusion.48
  192.2 1.4 fusion.49
  193.6 2.9 fusion.51
  196.6 1.4 compare_and_fusion.2
  198.1 2.3 fusion.48
  200.4 1.4 fusion.49
  201.8 2.9 fusion.51
  204.8 1.4 compare_and_fusion.2
  206.3 2.3 fusion.48
  208.6 1.4 fusion.49
  210.0 2.9 fusion.51
  213.0 1.4 compare_and_fusion.2
  214.5 2.3 fusion.48
  216.8 1.4 fusion.49
  218.2 2.9 fusion.51
  221.1 0.2 copy.26
  221.4 5.8 %convolution_convert_fusion = bf16[256,6144]{1,0:T(8,128)(2,1)} fusion(bf16[256,384]{0,1:T(8,128)(2,1)S(1)} %bitcast.74, bf16[384,6144]{1,0:T(8,128)(2,1)} %param.16), kind=kOutput, calls=%fused_computation.25 | convolution fusion | flops 1209532416 | bytes 8060928 | tf_op jit(solution)/shard_map/dot_general | solution.py:157
  227.2 77.1 %reduce-scatter.2.cloned.1.call-done = bf16[16,6144]{1,0:T(8,128)(2,1)} async-done(((bf16[256,6144]{1,0:T(8,128)(2,1)}), bf16[16,6144]{1,0:T(8,128)(2,1)}) %reduce-scatter.2.cloned.1.call-update) | async-done | bytes 196624 | tf_op jit(solution)/shard_map/reduce_scatter | solution.py:158
  (65 shorter events, 0.6 us)
Async XLA Ops:
  6.5 1.6 copy-start
  11.7 65.9 %all-to-all-start = ((bf16[128,128,128]{2,1,0:T(8,128)(2,1)}), bf16[128,128,128]{2,1,0:T(8,128)(2,1)}, u32[]{:S(2)}, u32[]{:S(2)}) async-start(bf16[128,128,128]{2,1,0:T(8,128)(2,1)} %bitcast.71), calls=%async_computation | async-start | bytes 8388608 | tf_op jit(solution)/shard_map/all_to_all | solution.py:70
  23.4 120.9 %all-gather.2.cloned.1.call-start = ((), (), s32[]{:S(2)}) async-start(), calls=%async_computation.3 | async-start | bytes 3342336 | tf_op jit(solution)/shard_map/all_gather | solution.py:37
  82.7 6.2 %copy-start.4 = (s32[32]{0:T(128)S(1)}, s32[32]{0:T(128)}, u32[]{:S(2)}) copy-start(s32[32]{0:T(128)} %param.20) | copy-start | bytes 388
  82.7 7.2 %copy-start.3 = (bf16[6144]{0:T(1024)(128)(2,1)S(1)}, bf16[6144]{0:T(1024)(128)(2,1)}, u32[]{:S(2)}) copy-start(bf16[6144]{0:T(1024)(128)(2,1)} %param.13) | copy-start | bytes 36868
  82.7 10.0 %copy-start.2 = (s32[256]{0:T(256)S(1)}, s32[256]{0:T(256)}, u32[]{:S(2)}) copy-start(s32[256]{0:T(256)} %param.21) | copy-start | bytes 3076
  82.7 72.9 %all-to-all-start.1 = ((bf16[128,128,128]{2,1,0:T(8,128)(2,1)}), bf16[128,128,128]{2,1,0:T(8,128)(2,1)}, u32[]{:S(2)}, u32[]{:S(2)}) async-start(bf16[128,128,128]{2,1,0:T(8,128)(2,1)} %bitcast.70), calls=%async_computation.1 | async-start | bytes 8388608 | tf_op jit(solution)/shard_map/all_to_all | solution.py:77
  88.7 215.7 %reduce-scatter.2.cloned.1.call-start = ((), (), s32[]{:S(2)}) async-start(), calls=%async_computation.4 | async-start | bytes 3342336 | tf_op jit(solution)/shard_map/reduce_scatter | solution.py:158
  146.9 3.9 %copy-start.1 = (bf16[256,6144]{1,0:T(8,128)(2,1)S(1)}, bf16[256,6144]{1,0:T(8,128)(2,1)}, u32[]{:S(2)}) copy-start(bf16[256,6144]{1,0:T(8,128)(2,1)} %all-gather.2.cloned.1.call-done) | copy-start | bytes 9437188
  150.6 4.8 %collective-permute-start = (bf16[256,128]{1,0:T(8,128)(2,1)S(1)}, bf16[256,128]{1,0:T(8,128)(2,1)S(1)}, u32[]{:S(2)}, u32[]{:S(2)}) collective-permute-start(bf16[256,128]{1,0:T(8,128)(2,1)S(1)} %convolution_convert_fusion.2), channel_id=1, source_target_pairs={{0,1},{1,0},{2,3},{3,2},{4,5},{5,4},{6,7},{7,6},{8,9},{9,8},{10,11... | collective-permute-start | bytes 196616 | tf_op jit(solution)/shard_map/ppermute | solution.py:17
Sparse Core Ops, SparseCore 0:
  26.4 117.9 all-gather.1
  227.3 76.9 reduce-scatter.1
where the time goes:
time: 312 us; the launch traced here: 311 us
  waiting for transfers between devices  179 us (57%)
  matrix products  55.7 us (18%)
  other arithmetic  26.4 us (8%)
  starting transfers between devices  18 us (6%)
  local copies, waits for them, and re-layouts  17.7 us (6%)
  between operations  13.6 us (4%)
    reduce_scatter x1, waiting for transfers between devices, per_device(): lax.psum_scatter(partials.astype(jnp.bfloat16), 'tp', scatter_dimension=0...  77.1 us
    all_gather x1, waiting for transfers between devices, per_device(): full_rows = lax.all_gather(hidden_in, 'tp', axis=1, tiled=True)  51.4 us
    all_to_all x1, waiting for transfers between devices, per_device(): lax.all_to_all(key_send.reshape(total_pieces, BLK, HD), ('seq', 'tp'), sp...  50 us
    dot_general x8, matrix products, attend_block(): jnp.einsum('rht,td->rhd', weights.astype(jnp.bfloat16), value_part, prefe...  23.5 us
    dot_general x8, matrix products, attend_block(): jnp.einsum('rhd,td->rht', queries, key_part, preferred_element_type=jnp.f...  18.5 us
    all_to_all x1, starting transfers between devices, per_device(): lax.all_to_all(key_send.reshape(total_pieces, BLK, HD), ('seq', 'tp'), sp...  11.7 us
    and x8, other arithmetic, attend_block(): (owner_part[None, :] == row_request[:, None]) & (position_part[None, :] <...  11.6 us
    reduce_sum x8, other arithmetic, attend_block(): run_sum = run_sum * factor + jnp.sum(weights, axis=2)  11 us
  transfers between devices with their start and end apart: 5, of which 3 were waited for; matrix products, arithmetic and copies ran while one was open for 8% of the time, Pallas kernels for 0%

commit v1 on v0

v1 whole, which is shorter than its diff:
```python
import functools

import jax
import jax.numpy as jnp
from jax import lax
from jax.experimental import pallas as pl
from jax.experimental.pallas import tpu as pltpu
from jax.sharding import PartitionSpec as P

MESH = pl.DeviceIdType.MESH
HD = 128
BLK = 128
ROWS = 256
FEAT = 384
SHARDS = 16
HEADS = 3
SLOTS = 64
CHUNK = 8
CHUNKS = 8
TILE = 512
TILES = 6
MASKED = -1e30
LOG2_SCALE = 1.4426950408889634 / HD**0.5


def ring_partner(y, o):
    return (3 - (y + 4 - o) % 4 + o) % 4


def body(
    hidden,
    gain,
    w_query,
    w_keyval,
    w_out,
    key_pool,
    value_pool,
    table,
    caps,
    row_req,
    out,
    hbuf,
    wqkv,
    wo,
    kbuf,
    vbuf,
    qaug,
    qown,
    kvown,
    acc,
    top,
    tot,
    osend,
    ssend,
    orecv,
    srecv,
    att,
    part,
    rs_a,
    rs_b,
    mid_a,
    mid_b,
    fin_a,
    fin_b,
    load_sem,
    ag_send,
    ag_recv,
    kv_send,
    k_recv,
    v_recv,
    q_send,
    q_recv,
    own_send,
    own_recv,
    o_send,
    o_recv,
    s_send,
    s_recv,
    rs1_send,
    rs1_recv,
    rs2_send,
    rs2_recv,
):
    seq = lax.axis_index("seq")
    tp = lax.axis_index("tp")
    x, y = tp // 4, tp % 4

    def remote(src, dst, send, recv, s, t):
        return pltpu.make_async_remote_copy(
            src, dst, send, recv, device_id=(s, t), device_id_type=MESH
        )

    own_load = pltpu.make_async_copy(hidden, hbuf.at[tp], load_sem.at[0])
    own_load.start()
    loads = [
        pltpu.make_async_copy(w_query, wqkv.at[:, pl.ds(0, 384)], load_sem.at[1]),
        pltpu.make_async_copy(w_keyval, wqkv.at[:, pl.ds(384, 128)], load_sem.at[2]),
        pltpu.make_async_copy(w_out, wo, load_sem.at[3]),
    ]
    for load in loads:
        load.start()

    barrier = pltpu.get_barrier_semaphore()

    def greet(s, t):
        pl.semaphore_signal(barrier, inc=1, device_id=(s, t), device_id_type=MESH)

    def greet_plane(i, carry):
        greet(seq, (tp + i) % 16)
        return carry

    lax.fori_loop(1, 16, greet_plane, 0)
    o_here, o_next = x % 2, (x + 1) % 2
    near = [
        (x, y),
        (x, ring_partner(y, 0)),
        (x, ring_partner(y, 1)),
        ((x + 3) % 4, y),
        ((x + 3) % 4, ring_partner(y, o_here)),
        ((x + 1) % 4, y),
        ((x + 1) % 4, ring_partner(y, o_next)),
    ]

    def greet_near(i, carry):
        for nx, ny in near:
            greet((seq + i) % 8, nx * 4 + ny)
        return carry

    lax.fori_loop(1, 8, greet_near, 0)
    own_load.wait()
    pl.semaphore_wait(barrier, 15 + 7 * 7)

    half = ROWS // 2
    for d in (1, 3, 2):
        remote(hbuf.at[tp], hbuf.at[tp], ag_send, ag_recv.at[tp, 0], seq, (x + d) % 4 * 4 + y).start()
        remote(hbuf.at[tp], hbuf.at[tp], ag_send, ag_recv.at[tp, 0], seq, x * 4 + (y + d) % 4).start()

    def send_chunk(ch, carry):
        u = ch % 2
        ix = ch // 4
        iy = (ch // 2) % 2
        kx = (x + 4 - (u + ix * (3 - 2 * u))) % 4
        o = kx % 2
        yy = (y + 4 - o) % 4
        ky = (yy // 2 + iy) % 2
        xd = (kx + u) % 4
        yd = iy * ((3 - yy + o) % 4) + (1 - iy) * y
        lanes = pl.ds(pl.multiple_of((2 * kx + ky) * HD, HD), HD)
        slot = ch * CHUNK + seq
        dest = xd * 4 + yd

        def send_one(i, c):
            g = (seq + i) % 8
            here = (i == 0) & (dest == tp)

            @pl.when(here)
            def _():
                pltpu.make_async_copy(
                    key_pool.at[g, :, lanes], kbuf.at[slot, :, pl.ds(0, HD)], k_recv.at[ch]
                ).start()
                pltpu.make_async_copy(
                    value_pool.at[g, :, lanes], vbuf.at[slot], v_recv.at[ch]
                ).start()

            @pl.when(jnp.logical_not(here))
            def _():
                remote(
                    key_pool.at[g, :, lanes], kbuf.at[slot, :, pl.ds(0, HD)],
                    kv_send.at[0], k_recv.at[ch], g, dest,
                ).start()
                remote(
                    value_pool.at[g, :, lanes], vbuf.at[slot],
                    kv_send.at[1], v_recv.at[ch], g, dest,
                ).start()

            return c

        return lax.fori_loop(0, 8, send_one, carry)

    lax.fori_loop(0, 2, send_chunk, 0)

    top_rows, low_rows = pl.ds(0, half), pl.ds(half, half)
    for d in (1, 3, 2):
        from_x = (x + 4 - d) % 4 * 4 + y
        pltpu.make_async_copy(hbuf.at[from_x], hbuf.at[from_x], ag_recv.at[from_x, 0]).wait()
        for e in (1, 3, 2):
            remote(
                hbuf.at[from_x, top_rows], hbuf.at[from_x, top_rows],
                ag_send, ag_recv.at[from_x, 0], seq, x * 4 + (y + e) % 4,
            ).start()
        from_y = x * 4 + (y + 4 - d) % 4
        pltpu.make_async_copy(hbuf.at[from_y], hbuf.at[from_y], ag_recv.at[from_y, 0]).wait()
        for e in (1, 3, 2):
            remote(
                hbuf.at[from_y, low_rows], hbuf.at[from_y, low_rows],
                ag_send, ag_recv.at[from_y, 1], seq, (x + e) % 4 * 4 + y,
            ).start()

    lax.fori_loop(2, CHUNKS, send_chunk, 0)

    lane = lax.broadcasted_iota(jnp.int32, (ROWS, HD), 1)
    onehot = jnp.where(row_req[...] == lane + seq * 4, 1.0, 0.0).astype(jnp.bfloat16)
    for u in range(2):
        for h in range(2 * HEADS):
            qaug[u, h, :, HD:] = onehot
    token = lax.broadcasted_iota(jnp.int32, (BLK, HD), 0)

    def mask_slot(slot, carry):
        ch, s = slot // 8, slot % 8
        u = ch % 2
        ix = ch // 4
        iy = (ch // 2) % 2
        kx = (x + 4 - u) % 4
        o = kx % 2
        xs = (x + 4 + ix * (2 * u - 1)) % 4
        ys = iy * ring_partner(y, o) + (1 - iy) * y
        block = (s * 16 + xs * 4 + ys) * 8 + seq
        valid = jnp.sum(jnp.where(table[...] == block, caps[...], 0), axis=0, keepdims=True)
        kbuf[slot, :, HD:] = jnp.where(token < valid, 0.0, MASKED).astype(jnp.bfloat16)
        return carry

    lax.fori_loop(0, SLOTS, mask_slot, 0)
    top[...] = jnp.full_like(top, 2 * MASKED)
    tot[...] = jnp.zeros_like(tot)
    acc[...] = jnp.zeros_like(acc)

    for d in (1, 3, 2):
        for e in (1, 3, 2):
            shard = (x + 4 - d) % 4 * 4 + (y + 4 - e) % 4
            pltpu.make_async_copy(
                hbuf.at[shard, top_rows], hbuf.at[shard, top_rows], ag_recv.at[shard, 0]
            ).wait()
            pltpu.make_async_copy(
                hbuf.at[shard, low_rows], hbuf.at[shard, low_rows], ag_recv.at[shard, 1]
            ).wait()

    def squares(t, total):
        wide = hbuf[t].astype(jnp.float32)
        return total + jnp.sum(wide * wide, axis=1, keepdims=True)

    square_sum = lax.fori_loop(0, SHARDS, squares, jnp.zeros((ROWS, 1), jnp.float32))
    factor = lax.rsqrt(square_sum / (SHARDS * FEAT) + 1e-5)
    loads[0].wait()
    loads[1].wait()

    def project(t, total):
        normed = (hbuf[t].astype(jnp.float32) * factor * gain[t].astype(jnp.float32)).astype(
            jnp.bfloat16
        )
        rows = pl.ds(pl.multiple_of(t * FEAT, FEAT), FEAT)
        return total + jnp.dot(normed, wqkv[rows, :], preferred_element_type=jnp.float32)

    projected = lax.fori_loop(0, SHARDS, project, jnp.zeros((ROWS, 512), jnp.float32)).astype(
        jnp.bfloat16
    )
    for h in range(HEADS):
        qown[h] = projected[:, h * HD : (h + 1) * HD]
    kvown[tp % 2] = projected[:, HEADS * HD :]

    own_copy = remote(
        kvown.at[tp % 2], kvown.at[tp % 2], own_send, own_recv.at[tp % 2], seq, tp + 1 - 2 * (tp % 2)
    )
    own_half = tp % 2

    def q_copies(u, j):
        t = (x + u) % 4 * 4 + (y // 2 * 2 + j + o_here) % 4
        dst = qaug.at[u, pl.ds(own_half * HEADS, HEADS), :, pl.ds(0, HD)]
        there = remote(qown, dst, q_send.at[u, j], q_recv.at[u, own_half], seq, t)
        here = pltpu.make_async_copy(qown, dst, q_recv.at[u, own_half])
        return t == tp, here, there

    for u in range(2):
        for j in range(2):
            same, here, there = q_copies(u, j)
            pl.when(same)(here.start)
            pl.when(jnp.logical_not(same))(there.start)
    own_copy.start()
    for u in range(2):
        for part_half in range(2):
            dst = qaug.at[u, pl.ds(part_half * HEADS, HEADS), :, pl.ds(0, HD)]
            pltpu.make_async_copy(dst, dst, q_recv.at[u, part_half]).wait()

    def attend_chunk(ch, carry):
        u = ch % 2
        slots = pl.ds(pl.multiple_of(ch * CHUNK, CHUNK), CHUNK)
        k_dst = kbuf.at[slots, :, pl.ds(0, HD)]
        pltpu.make_async_copy(k_dst, k_dst, k_recv.at[ch]).wait()
        pltpu.make_async_copy(vbuf.at[slots], vbuf.at[slots], v_recv.at[ch]).wait()

        def attend_head(h, c):
            keys = kbuf[slots].reshape(CHUNK * BLK, 2 * HD)
            values = vbuf[slots].reshape(CHUNK * BLK, HD)
            scores = lax.dot_general(
                qaug[u, h], keys, (((1,), (1,)), ((), ())), preferred_element_type=jnp.float32
            )
            old = top[u, h]
            new = jnp.maximum(old, jnp.max(scores, axis=1, keepdims=True))
            shrink = jnp.exp2((old - new) * LOG2_SCALE)
            weights = jnp.exp2(scores * LOG2_SCALE - new[:, :1] * LOG2_SCALE)
            top[u, h] = new
            tot[u, h] = tot[u, h] * shrink + jnp.sum(weights, axis=1, keepdims=True)
            acc[u, h] = acc[u, h] * shrink + jnp.dot(
                weights.astype(jnp.bfloat16), values, preferred_element_type=jnp.float32
            )
            return c

        return lax.fori_loop(0, 2 * HEADS, attend_head, carry)

    lax.fori_loop(0, CHUNKS, attend_chunk, 0)

    def o_copies(u, to):
        kx = (x + 4 - u) % 4
        o = kx % 2
        yy = (y + 4 - o) % 4
        t = kx * 4 + yy // 2 * 2 + to
        index = u * 2 + yy % 2
        o_src, o_dst = osend.at[u, to], orecv.at[index]
        s_src, s_dst = ssend.at[u, to], srecv.at[pl.ds(pl.multiple_of(index * 8, 8), 8)]
        return (
            t == tp,
            pltpu.make_async_copy(o_src, o_dst, o_recv.at[index]),
            remote(o_src, o_dst, o_send.at[u, to], o_recv.at[index], seq, t),
            pltpu.make_async_copy(s_src, s_dst, s_recv.at[index]),
            remote(s_src, s_dst, s_send.at[u, to], s_recv.at[index], seq, t),
        )

    srecv[pl.ds(32, 96), :] = jnp.zeros((96, ROWS), jnp.float32)
    for u in range(2):
        for to in range(2):
            stats = jnp.zeros((ROWS, HD), jnp.float32)
            for h in range(HEADS):
                stats = jnp.where(lane == h, top[u, to * HEADS + h], stats)
                stats = jnp.where(lane == HEADS + h, tot[u, to * HEADS + h], stats)
                osend[u, to, h] = acc[u, to * HEADS + h].astype(jnp.bfloat16)
            ssend[u, to] = stats.T[:8]
            same, o_here_copy, o_there, s_here_copy, s_there = o_copies(u, to)

            @pl.when(same)
            def _():
                o_here_copy.start()
                s_here_copy.start()

            @pl.when(jnp.logical_not(same))
            def _():
                o_there.start()
                s_there.start()

    own_copy.wait_send()
    other = 1 - tp % 2
    pltpu.make_async_copy(kvown.at[other], kvown.at[other], own_recv.at[other]).wait()
    own_key = kvown[0].astype(jnp.float32)
    own_value = kvown[1].astype(jnp.float32)
    self_scores = [
        jnp.sum(qown[h].astype(jnp.float32) * own_key, axis=1, keepdims=True) for h in range(HEADS)
    ]
    for i in range(4):
        pltpu.make_async_copy(orecv.at[i], orecv.at[i], o_recv.at[i]).wait()
        s_dst = srecv.at[pl.ds(i * 8, 8)]
        pltpu.make_async_copy(s_dst, s_dst, s_recv.at[i]).wait()
    stats = srecv[...].T
    for h in range(HEADS):
        tops = [stats[:, i * 8 + h : i * 8 + h + 1] for i in range(4)]
        best = self_scores[h]
        for one in tops:
            best = jnp.maximum(best, one)
        own_weight = jnp.exp2((self_scores[h] - best) * LOG2_SCALE)
        total = own_weight
        numer = own_weight.astype(jnp.bfloat16).astype(jnp.float32) * own_value
        for i in range(4):
            scale = jnp.exp2((tops[i] - best) * LOG2_SCALE)
            total = total + scale * stats[:, i * 8 + HEADS + h : i * 8 + HEADS + h + 1]
            numer = numer + scale * orecv[i, h].astype(jnp.float32)
        att[:, h * HD : (h + 1) * HD] = (numer / total).astype(jnp.bfloat16)

    loads[2].wait()

    def columns(tile, first=0):
        return pl.ds(pl.multiple_of(first + tile * TILE, TILE), TILE)

    def project_out(tile, carry):
        for side in range(2):
            cols = columns(tile, side * TILES * TILE)
            part[:, :, :, cols] = (
                jnp.dot(att[...], wo[:, cols], preferred_element_type=jnp.float32)
                .astype(jnp.bfloat16)
                .reshape(4, 4, 16, TILE)
            )
            for d in (1, 3, 2):
                if side == 0:
                    src, t = part.at[(x + d) % 4, :, :, cols], (x + d) % 4 * 4 + y
                else:
                    src, t = part.at[:, (y + d) % 4, :, cols], x * 4 + (y + d) % 4
                dst = (rs_a, rs_b)[side].at[d - 1, :, :, columns(tile)]
                remote(
                    src, dst, rs1_send.at[side], rs1_recv.at[side, tile, d - 1], seq, t
                ).start()
        return carry

    lax.fori_loop(0, TILES, project_out, 0)

    def sum_first(tile, carry):
        for side in range(2):
            cols = columns(tile, side * TILES * TILE)
            here = columns(tile)
            landed = (rs_a, rs_b)[side]
            mid = (mid_a, mid_b)[side]
            if side == 0:
                total = part[x, :, :, cols].astype(jnp.float32)
            else:
                total = part[:, y, :, cols].astype(jnp.float32)
            for d in range(3):
                dst = landed.at[d, :, :, here]
                pltpu.make_async_copy(dst, dst, rs1_recv.at[side, tile, d]).wait()
                total = total + landed[d, :, :, here].astype(jnp.float32)
            mid[:, :, here] = total.astype(jnp.bfloat16)
            for d in (1, 3, 2):
                if side == 0:
                    src, t = mid.at[(y + d) % 4, :, here], x * 4 + (y + d) % 4
                else:
                    src, t = mid.at[(x + d) % 4, :, here], (x + d) % 4 * 4 + y
                dst = (fin_a, fin_b)[side].at[d - 1, :, here]
                remote(
                    src, dst, rs2_send.at[side], rs2_recv.at[side, tile, d - 1], seq, t
                ).start()
        return carry

    lax.fori_loop(0, TILES, sum_first, 0)

    def sum_last(tile, carry):
        for side in range(2):
            here = columns(tile)
            landed = (fin_a, fin_b)[side]
            if side == 0:
                total = mid_a[y, :, here].astype(jnp.float32)
            else:
                total = mid_b[x, :, here].astype(jnp.float32)
            for d in range(3):
                dst = landed.at[d, :, here]
                pltpu.make_async_copy(dst, dst, rs2_recv.at[side, tile, d]).wait()
                total = total + landed[d, :, here].astype(jnp.float32)
            out[:, columns(tile, side * TILES * TILE)] = total.astype(jnp.bfloat16)
        return carry

    lax.fori_loop(0, TILES, sum_last, 0)

    sent = hbuf.at[pl.ds(0, SHARDS - 1)]
    pltpu.make_async_copy(sent, sent, ag_send).wait()
    sent = kbuf.at[pl.ds(0, SLOTS - 2), :, pl.ds(0, HD)]
    pltpu.make_async_copy(sent, sent, kv_send.at[0]).wait()
    sent = vbuf.at[pl.ds(0, SLOTS - 2)]
    pltpu.make_async_copy(sent, sent, kv_send.at[1]).wait()
    for u in range(2):
        for j in range(2):
            same, _, there = q_copies(u, j)
            pl.when(jnp.logical_not(same))(there.wait_send)
            same, _, o_there, _, s_there = o_copies(u, j)

            @pl.when(jnp.logical_not(same))
            def _():
                o_there.wait_send()
                s_there.wait_send()

    for side in range(2):
        sent = (rs_a, rs_b)[side]
        pltpu.make_async_copy(sent, sent, rs1_send.at[side]).wait()
        sent = (fin_a, fin_b)[side]
        pltpu.make_async_copy(sent, sent, rs2_send.at[side]).wait()


def per_device(
    hidden_in,
    norm_gain,
    w_query,
    w_keyval,
    w_out,
    key_pool,
    value_pool,
    block_table,
    prefix_lengths,
    row_request,
):
    seq = lax.axis_index("seq")
    table = lax.dynamic_slice_in_dim(block_table, seq * 4, 4, 0)
    lengths = lax.dynamic_slice_in_dim(prefix_lengths, seq * 4, 4, 0)
    starts = jnp.arange(64, dtype=jnp.int32)[:, None] * BLK
    caps = jnp.clip(lengths[None, :] - starts, 0, BLK)
    table = jnp.pad(table.T, ((0, 0), (0, HD - 4)), constant_values=-1)
    caps = jnp.pad(caps, ((0, 0), (0, HD - 4)))
    bf16, f32 = jnp.bfloat16, jnp.float32
    vmem = functools.partial(pltpu.VMEM)
    dma = pltpu.SemaphoreType.DMA
    any_spec = pl.BlockSpec(memory_space=pl.ANY)
    vmem_spec = pl.BlockSpec(memory_space=pltpu.VMEM)
    return pl.pallas_call(
        body,
        out_shape=jax.ShapeDtypeStruct((16, 6144), bf16),
        in_specs=[any_spec, vmem_spec] + [any_spec] * 5 + [vmem_spec] * 3,
        out_specs=vmem_spec,
        scratch_shapes=[
            vmem((SHARDS, ROWS, FEAT), bf16),
            vmem((SHARDS * FEAT, 512), bf16),
            vmem((FEAT, 6144), bf16),
            vmem((SLOTS, BLK, 2 * HD), bf16),
            vmem((SLOTS, BLK, HD), bf16),
            vmem((2, 2 * HEADS, ROWS, 2 * HD), bf16),
            vmem((HEADS, ROWS, HD), bf16),
            vmem((2, ROWS, HD), bf16),
            vmem((2, 2 * HEADS, ROWS, HD), f32),
            vmem((2, 2 * HEADS, ROWS, HD), f32),
            vmem((2, 2 * HEADS, ROWS, HD), f32),
            vmem((2, 2, HEADS, ROWS, HD), bf16),
            vmem((2, 2, 8, ROWS), f32),
            vmem((4, HEADS, ROWS, HD), bf16),
            vmem((128, ROWS), f32),
            vmem((ROWS, FEAT), bf16),
            vmem((4, 4, 16, 6144), bf16),
            vmem((3, 4, 16, 3072), bf16),
            vmem((3, 4, 16, 3072), bf16),
            vmem((4, 16, 3072), bf16),
            vmem((4, 16, 3072), bf16),
            vmem((3, 16, 3072), bf16),
            vmem((3, 16, 3072), bf16),
            dma((4,)),
            dma,
            dma((SHARDS, 2)),
            dma((2,)),
            dma((CHUNKS,)),
            dma((CHUNKS,)),
            dma((2, 2)),
            dma((2, 2)),
            dma,
            dma((2,)),
            dma((2, 2)),
            dma((4,)),
            dma((2, 2)),
            dma((4,)),
            dma((2,)),
            dma((2, TILES, 3)),
            dma((2,)),
            dma((2, TILES, 3)),
        ],
        compiler_params=pltpu.CompilerParams(
            collective_id=0, has_side_effects=True, vmem_limit_bytes=56 << 20
        ),
        cost_estimate=pl.CostEstimate(
            flops=10_000_000_000, bytes_accessed=20_000_000, transcendentals=13_000_000
        ),
    )(
        hidden_in,
        norm_gain.reshape(SHARDS, 1, FEAT),
        w_query,
        w_keyval,
        w_out,
        key_pool,
        value_pool,
        table,
        caps,
        row_request.reshape(ROWS, 1),
    )


def solution(mesh):
    return jax.shard_map(
        per_device,
        mesh=mesh,
        in_specs=(
            P("seq", "tp"),
            P(),
            P(None, "tp"),
            P(None, "tp"),
            P("tp", None),
            P(("seq", "tp"), None, None),
            P(("seq", "tp"), None, None),
            P(),
            P(),
            P("seq"),
        ),
        out_specs=P(("seq", "tp"), None),
        check_vma=False,
    )
```

time: 312 us -> 174 us (0.56)
  waiting for transfers between devices: 179 us -> 0 us
  Pallas kernels: 0 us -> 167 us
  matrix products: 55.7 us -> 0 us
  other arithmetic: 26.4 us -> 0.08 us
  starting transfers between devices: 18 us -> 0 us
  between operations: 13.6 us -> 0.02 us
  local copies, waits for them, and re-layouts: 17.7 us -> 6.5 us
    pallas_call x0 -> x1, Pallas kernels: none -> 167 us  [per_device(): pl.pallas_call(body, out_shape=jax.ShapeDtypeStruct((16, 6144), bf16), in...]
    reduce_scatter x1 -> x0, waiting for transfers between devices: 77.1 us -> none  [per_device(): lax.psum_scatter(partials.astype(jnp.bfloat16), 'tp', scatter_dimension=0...]
    dot_general x19 -> x0, matrix products: 55.7 us -> none  [the longest x8 23.5 us: attend_block(): jnp.einsum('rht,td->rhd', weights.astype(jnp.bfloat16), value_part, prefe...]
    all_gather x1 -> x0, waiting for transfers between devices: 51.4 us -> none  [per_device(): full_rows = lax.all_gather(hidden_in, 'tp', axis=1, tiled=True)]
    all_to_all x2 -> x0, waiting for transfers between devices: 50 us -> none  [the longest x1 50 us: per_device(): lax.all_to_all(key_send.reshape(total_pieces, BLK, HD), ('seq', 'tp'), sp...]
    all_to_all x2 -> x0, starting transfers between devices: 17.6 us -> none  [the longest x1 11.7 us: per_device(): lax.all_to_all(key_send.reshape(total_pieces, BLK, HD), ('seq', 'tp'), sp...]
    reduce_sum x10 -> x0, other arithmetic: 13.7 us -> none  [the longest x8 11 us: attend_block(): run_sum = run_sum * factor + jnp.sum(weights, axis=2)]
    and x8 -> x0, other arithmetic: 11.6 us -> none  [attend_block(): (owner_part[None, :] == row_request[:, None]) & (position_part[None, :] <...]
  transfers between devices with their start and end apart: 5 -> 0, of which waited for: 3 -> 0; matrix products, arithmetic and copies ran while one was open for 8% -> 0% of each run, Pallas kernels for 0% -> 0%
where the time goes in v1:
time: 174 us; the launch traced here: 173 us
  Pallas kernels  167 us (96%)
  local copies, waits for them, and re-layouts  6.5 us (4%)
    pallas_call x1, Pallas kernels, per_device(): pl.pallas_call(body, out_shape=jax.ShapeDtypeStruct((16, 6144), bf16), in...  167 us

profile of v1, /device:TPU:0, one launch (start us, length us, event | category | flops | bytes accessed | tf_op | source)
XLA Modules:
  0.0 173.5 jit_solution(7172908251387591929)
XLA Ops:
  0.0 0.0 copy-start
  0.0 0.7 dynamic_slice.7
  0.7 0.0 copy-done
  0.8 1.3 reshape.14.gain
  2.1 0.1 copy.19
  2.2 0.6 pad.7.table
  2.8 0.1 subtract_clamp_fusion
  2.9 0.6 pad.8.caps
  3.5 1.5 copy.18.row_req
  5.0 166.9 %shard_map.100 = bf16[16,6144]{1,0:T(8,128)(2,1)} custom-call(bf16[256,384]{1,0:T(8,128)(2,1)} %hidden.1, bf16[16,1,384]{2,1,0:T(2,128)(2,1)} %reshape.14.gain, bf16[6144,384]{1,0:T(8,128)(2,1)} %w_query.1, bf16[6144,128]{1,0:T(8,128)(2,1)} %w_keyval.1, bf16[384,6144]{1,0:T(8,128)(2,1)} %w_out.1, bf16[8,128,1024]{2,1,0:T(8,128)(2,1)} %key_pool.1, ...), custom_call_target="tpu_custom_call" | custom-call | flops 10000000000 | bytes 20000000 | tf_op jit(solution)/shard_map/pallas_call | solution.py:494
  171.9 1.6 copy.24
  (2 shorter events, 0.0 us)
Async XLA Ops:
  0.0 0.8 copy-start

commit v2 on v1

--- a/solution.py
+++ b/solution.py
@@ -23,8 +23,8 @@
 LOG2_SCALE = 1.4426950408889634 / HD**0.5
 
 
-def ring_partner(y, o):
-    return (3 - (y + 4 - o) % 4 + o) % 4
+def ring_partner(y, shift):
+    return (7 - (y + 4 - shift) % 4 + shift) % 4
 
 
 def body(
@@ -36,7 +36,7 @@
     key_pool,
     value_pool,
     table,
-    caps,
+    lengths,
     row_req,
     out,
     hbuf,
@@ -54,6 +54,13 @@
     ssend,
     orecv,
     srecv,
+    squares_own,
+    squares_x,
+    squares_mid,
+    squares_y,
+    table_wide,
+    table_cols,
+    caps,
     att,
     part,
     rs_a,
@@ -63,6 +70,10 @@
     fin_a,
     fin_b,
     load_sem,
+    column_sem,
+    plane_sem,
+    sq_send,
+    sq_recv,
     ag_send,
     ag_recv,
     kv_send,
@@ -84,11 +95,28 @@
     seq = lax.axis_index("seq")
     tp = lax.axis_index("tp")
     x, y = tp // 4, tp % 4
+    sign = 1 - 2 * (seq % 2)
 
     def remote(src, dst, send, recv, s, t):
         return pltpu.make_async_remote_copy(
             src, dst, send, recv, device_id=(s, t), device_id_type=MESH
         )
+
+    def signal(sem, s, t):
+        pl.semaphore_signal(sem, inc=1, device_id=(s, t), device_id_type=MESH)
+
+    def x_peer(d):
+        return (x + d) % 4 * 4 + y
+
+    def y_peer(d):
+        return x * 4 + (y + d) % 4
+
+    barrier = pltpu.get_barrier_semaphore()
+    for d in (1, 3, 2):
+        signal(barrier, seq, x_peer(d))
+        signal(barrier, seq, y_peer(d))
+    for i in range(1, 8):
+        signal(barrier, (seq + i) % 8, tp)
 
     own_load = pltpu.make_async_copy(hidden, hbuf.at[tp], load_sem.at[0])
     own_load.start()
@@ -99,58 +127,40 @@
     ]
     for load in loads:
         load.start()
-
-    barrier = pltpu.get_barrier_semaphore()
-
-    def greet(s, t):
-        pl.semaphore_signal(barrier, inc=1, device_id=(s, t), device_id_type=MESH)
-
-    def greet_plane(i, carry):
-        greet(seq, (tp + i) % 16)
-        return carry
-
-    lax.fori_loop(1, 16, greet_plane, 0)
-    o_here, o_next = x % 2, (x + 1) % 2
-    near = [
-        (x, y),
-        (x, ring_partner(y, 0)),
-        (x, ring_partner(y, 1)),
-        ((x + 3) % 4, y),
-        ((x + 3) % 4, ring_partner(y, o_here)),
-        ((x + 1) % 4, y),
-        ((x + 1) % 4, ring_partner(y, o_next)),
-    ]
-
-    def greet_near(i, carry):
-        for nx, ny in near:
-            greet((seq + i) % 8, nx * 4 + ny)
-        return carry
-
-    lax.fori_loop(1, 8, greet_near, 0)
     own_load.wait()
-    pl.semaphore_wait(barrier, 15 + 7 * 7)
+    wide = hbuf[tp].astype(jnp.float32)
+    own_sum = jnp.broadcast_to(jnp.sum(wide * wide, axis=1, keepdims=True), (ROWS, HD))
+    squares_own[...] = own_sum.T[:8]
+    pl.semaphore_wait(barrier, 13)
+    for d in (1, 3, 2):
+        signal(column_sem, seq, y_peer(d))
 
     half = ROWS // 2
     for d in (1, 3, 2):
-        remote(hbuf.at[tp], hbuf.at[tp], ag_send, ag_recv.at[tp, 0], seq, (x + d) % 4 * 4 + y).start()
-        remote(hbuf.at[tp], hbuf.at[tp], ag_send, ag_recv.at[tp, 0], seq, x * 4 + (y + d) % 4).start()
+        remote(
+            squares_own, squares_x.at[d - 1], sq_send.at[0], sq_recv.at[0, d - 1], seq, x_peer(d)
+        ).start()
+    for d in (1, 3, 2):
+        remote(hbuf.at[tp], hbuf.at[tp], ag_send, ag_recv.at[tp, 0], seq, x_peer(d)).start()
+        remote(hbuf.at[tp], hbuf.at[tp], ag_send, ag_recv.at[tp, 0], seq, y_peer(d)).start()
 
     def send_chunk(ch, carry):
         u = ch % 2
         ix = ch // 4
         iy = (ch // 2) % 2
-        kx = (x + 4 - (u + ix * (3 - 2 * u))) % 4
-        o = kx % 2
-        yy = (y + 4 - o) % 4
-        ky = (yy // 2 + iy) % 2
-        xd = (kx + u) % 4
-        yd = iy * ((3 - yy + o) % 4) + (1 - iy) * y
-        lanes = pl.ds(pl.multiple_of((2 * kx + ky) * HD, HD), HD)
         slot = ch * CHUNK + seq
-        dest = xd * 4 + yd
+        back = u + ix * (3 - 2 * u)
 
         def send_one(i, c):
             g = (seq + i) % 8
+            turn = 1 - 2 * (g % 2)
+            kx = (x + 4 - turn * back) % 4
+            shift = (kx % 2) * turn
+            ky = ((y + 4 - shift) % 4 // 2 + iy) % 2
+            xd = (kx + 4 + turn * u) % 4
+            yd = iy * ring_partner(y, shift) + (1 - iy) * y
+            lanes = pl.ds(pl.multiple_of((2 * kx + ky) * HD, HD), HD)
+            dest = xd * 4 + yd
             here = (i == 0) & (dest == tp)
 
             @pl.when(here)
@@ -179,30 +189,58 @@
 
     lax.fori_loop(0, 2, send_chunk, 0)
 
+    def landed(ref, sem):
+        pltpu.make_async_copy(ref, ref, sem).wait()
+
+    square_sums = squares_own[...]
+    for d in range(3):
+        landed(squares_x.at[d], sq_recv.at[0, d])
+        square_sums = square_sums + squares_x[d]
+    squares_mid[...] = square_sums
+    for d in (1, 3, 2):
+        remote(
+            squares_mid, squares_y.at[d - 1], sq_send.at[1], sq_recv.at[1, d - 1], seq, y_peer(d)
+        ).start()
+
+    pl.semaphore_wait(column_sem, 3)
+    signal(plane_sem, seq, x_peer(1))
+    signal(plane_sem, seq, x_peer(3))
+
     top_rows, low_rows = pl.ds(0, half), pl.ds(half, half)
     for d in (1, 3, 2):
-        from_x = (x + 4 - d) % 4 * 4 + y
-        pltpu.make_async_copy(hbuf.at[from_x], hbuf.at[from_x], ag_recv.at[from_x, 0]).wait()
+        from_x = x_peer(4 - d)
+        landed(hbuf.at[from_x], ag_recv.at[from_x, 0])
         for e in (1, 3, 2):
             remote(
                 hbuf.at[from_x, top_rows], hbuf.at[from_x, top_rows],
-                ag_send, ag_recv.at[from_x, 0], seq, x * 4 + (y + e) % 4,
+                ag_send, ag_recv.at[from_x, 0], seq, y_peer(e),
             ).start()
-        from_y = x * 4 + (y + 4 - d) % 4
-        pltpu.make_async_copy(hbuf.at[from_y], hbuf.at[from_y], ag_recv.at[from_y, 0]).wait()
+        from_y = y_peer(4 - d)
+        landed(hbuf.at[from_y], ag_recv.at[from_y, 0])
         for e in (1, 3, 2):
             remote(
                 hbuf.at[from_y, low_rows], hbuf.at[from_y, low_rows],
-                ag_send, ag_recv.at[from_y, 1], seq, (x + e) % 4 * 4 + y,
+                ag_send, ag_recv.at[from_y, 1], seq, x_peer(e),
             ).start()
 
+    pl.semaphore_wait(plane_sem, 2)
     lax.fori_loop(2, CHUNKS, send_chunk, 0)
 
     lane = lax.broadcasted_iota(jnp.int32, (ROWS, HD), 1)
-    onehot = jnp.where(row_req[...] == lane + seq * 4, 1.0, 0.0).astype(jnp.bfloat16)
+    first_request = seq // 2 * 8
+    requests = jnp.broadcast_to(row_req[...], (HD, ROWS)).T
+    onehot = jnp.where(requests == lane + first_request, 1.0, 0.0).astype(jnp.bfloat16)
     for u in range(2):
         for h in range(2 * HEADS):
             qaug[u, h, :, HD:] = onehot
+    table_wide[...] = jnp.full_like(table_wide, -1)
+    table_wide[:8, :64] = table[pl.ds(pl.multiple_of(first_request, 8), 8), :]
+    table_cols[...] = table_wide[...].T[:64]
+    table_lane = lax.broadcasted_iota(jnp.int32, (64, HD), 1)
+    ends = jnp.zeros((64, HD), jnp.int32)
+    for r in range(8):
+        ends = jnp.where(table_lane == r, lengths[first_request + r], ends)
+    caps[...] = jnp.clip(ends - BLK * lax.broadcasted_iota(jnp.int32, (64, HD), 0), 0, BLK)
     token = lax.broadcasted_iota(jnp.int32, (BLK, HD), 0)
 
     def mask_slot(slot, carry):
@@ -210,12 +248,11 @@
         u = ch % 2
         ix = ch // 4
         iy = (ch // 2) % 2
-        kx = (x + 4 - u) % 4
-        o = kx % 2
-        xs = (x + 4 + ix * (2 * u - 1)) % 4
-        ys = iy * ring_partner(y, o) + (1 - iy) * y
+        shift = ((x + 4 - sign * u) % 4) % 2 * sign
+        xs = (x + 4 + sign * ix * (2 * u - 1)) % 4
+        ys = iy * ring_partner(y, shift) + (1 - iy) * y
         block = (s * 16 + xs * 4 + ys) * 8 + seq
-        valid = jnp.sum(jnp.where(table[...] == block, caps[...], 0), axis=0, keepdims=True)
+        valid = jnp.sum(jnp.where(table_cols[...] == block, caps[...], 0), axis=0, keepdims=True)
         kbuf[slot, :, HD:] = jnp.where(token < valid, 0.0, MASKED).astype(jnp.bfloat16)
         return carry
 
@@ -224,35 +261,35 @@
     tot[...] = jnp.zeros_like(tot)
     acc[...] = jnp.zeros_like(acc)
 
-    for d in (1, 3, 2):
-        for e in (1, 3, 2):
-            shard = (x + 4 - d) % 4 * 4 + (y + 4 - e) % 4
-            pltpu.make_async_copy(
-                hbuf.at[shard, top_rows], hbuf.at[shard, top_rows], ag_recv.at[shard, 0]
-            ).wait()
-            pltpu.make_async_copy(
-                hbuf.at[shard, low_rows], hbuf.at[shard, low_rows], ag_recv.at[shard, 1]
-            ).wait()
-
-    def squares(t, total):
-        wide = hbuf[t].astype(jnp.float32)
-        return total + jnp.sum(wide * wide, axis=1, keepdims=True)
-
-    square_sum = lax.fori_loop(0, SHARDS, squares, jnp.zeros((ROWS, 1), jnp.float32))
-    factor = lax.rsqrt(square_sum / (SHARDS * FEAT) + 1e-5)
+    for d in range(3):
+        landed(squares_y.at[d], sq_recv.at[1, d])
+        square_sums = square_sums + squares_y[d]
+    square_cols = jnp.broadcast_to(square_sums[:1], (HD, ROWS)).T
+    factor = lax.rsqrt(square_cols[:, :1] / (SHARDS * FEAT) + 1e-5)
     loads[0].wait()
     loads[1].wait()
 
     def project(t, total):
-        normed = (hbuf[t].astype(jnp.float32) * factor * gain[t].astype(jnp.float32)).astype(
-            jnp.bfloat16
-        )
-        rows = pl.ds(pl.multiple_of(t * FEAT, FEAT), FEAT)
-        return total + jnp.dot(normed, wqkv[rows, :], preferred_element_type=jnp.float32)
-
-    projected = lax.fori_loop(0, SHARDS, project, jnp.zeros((ROWS, 512), jnp.float32)).astype(
-        jnp.bfloat16
-    )
+        feats = pl.ds(pl.multiple_of(t * FEAT, FEAT), FEAT)
+        normed = (
+            hbuf[t].astype(jnp.float32) * factor * gain[:, feats].astype(jnp.float32)
+        ).astype(jnp.bfloat16)
+        return total + jnp.dot(normed, wqkv[feats, :], preferred_element_type=jnp.float32)
+
+    def project_line(i, total):
+        along = i // 4
+        d = i % 4
+        return project((x + (1 - along) * d) % 4 * 4 + (y + along * d) % 4, total)
+
+    def project_far(i, total):
+        shard = (x + 1 + i // 3) % 4 * 4 + (y + 1 + i % 3) % 4
+        landed(hbuf.at[shard, top_rows], ag_recv.at[shard, 0])
+        landed(hbuf.at[shard, low_rows], ag_recv.at[shard, 1])
+        return project(shard, total)
+
+    projected = lax.fori_loop(0, 4, project_line, jnp.zeros((ROWS, 512), jnp.float32))
+    projected = lax.fori_loop(5, 8, project_line, projected)
+    projected = lax.fori_loop(0, 9, project_far, projected).astype(jnp.bfloat16)
     for h in range(HEADS):
         qown[h] = projected[:, h * HD : (h + 1) * HD]
     kvown[tp % 2] = projected[:, HEADS * HD :]
@@ -263,7 +300,7 @@
     own_half = tp % 2
 
     def q_copies(u, j):
-        t = (x + u) % 4 * 4 + (y // 2 * 2 + j + o_here) % 4
+        t = (x + 4 + sign * u) % 4 * 4 + (y // 2 * 2 + j + 4 + x % 2 * sign) % 4
         dst = qaug.at[u, pl.ds(own_half * HEADS, HEADS), :, pl.ds(0, HD)]
         there = remote(qown, dst, q_send.at[u, j], q_recv.at[u, own_half], seq, t)
         here = pltpu.make_async_copy(qown, dst, q_recv.at[u, own_half])
@@ -280,42 +317,15 @@
             dst = qaug.at[u, pl.ds(part_half * HEADS, HEADS), :, pl.ds(0, HD)]
             pltpu.make_async_copy(dst, dst, q_recv.at[u, part_half]).wait()
 
-    def attend_chunk(ch, carry):
-        u = ch % 2
-        slots = pl.ds(pl.multiple_of(ch * CHUNK, CHUNK), CHUNK)
-        k_dst = kbuf.at[slots, :, pl.ds(0, HD)]
-        pltpu.make_async_copy(k_dst, k_dst, k_recv.at[ch]).wait()
-        pltpu.make_async_copy(vbuf.at[slots], vbuf.at[slots], v_recv.at[ch]).wait()
-
-        def attend_head(h, c):
-            keys = kbuf[slots].reshape(CHUNK * BLK, 2 * HD)
-            values = vbuf[slots].reshape(CHUNK * BLK, HD)
-            scores = lax.dot_general(
-                qaug[u, h], keys, (((1,), (1,)), ((), ())), preferred_element_type=jnp.float32
-            )
-            old = top[u, h]
-            new = jnp.maximum(old, jnp.max(scores, axis=1, keepdims=True))
-            shrink = jnp.exp2((old - new) * LOG2_SCALE)
-            weights = jnp.exp2(scores * LOG2_SCALE - new[:, :1] * LOG2_SCALE)
-            top[u, h] = new
-            tot[u, h] = tot[u, h] * shrink + jnp.sum(weights, axis=1, keepdims=True)
-            acc[u, h] = acc[u, h] * shrink + jnp.dot(
-                weights.astype(jnp.bfloat16), values, preferred_element_type=jnp.float32
-            )
-            return c
-
-        return lax.fori_loop(0, 2 * HEADS, attend_head, carry)
-
-    lax.fori_loop(0, CHUNKS, attend_chunk, 0)
-
     def o_copies(u, to):
-        kx = (x + 4 - u) % 4
-        o = kx % 2
-        yy = (y + 4 - o) % 4
+        kx = (x + 4 - sign * u) % 4
+        shift = kx % 2 * sign
+        yy = (y + 4 - shift) % 4
         t = kx * 4 + yy // 2 * 2 + to
         index = u * 2 + yy % 2
         o_src, o_dst = osend.at[u, to], orecv.at[index]
-        s_src, s_dst = ssend.at[u, to], srecv.at[pl.ds(pl.multiple_of(index * 8, 8), 8)]
+        s_src = ssend.at[u, to]
+        s_dst = srecv.at[pl.ds(pl.multiple_of(index * 8, 8), 8)]
         return (
             t == tp,
             pltpu.make_async_copy(o_src, o_dst, o_recv.at[index]),
@@ -325,13 +335,15 @@
         )
 
     srecv[pl.ds(32, 96), :] = jnp.zeros((96, ROWS), jnp.float32)
-    for u in range(2):
+
+    def send_partials(u):
         for to in range(2):
             stats = jnp.zeros((ROWS, HD), jnp.float32)
             for h in range(HEADS):
-                stats = jnp.where(lane == h, top[u, to * HEADS + h], stats)
-                stats = jnp.where(lane == HEADS + h, tot[u, to * HEADS + h], stats)
-                osend[u, to, h] = acc[u, to * HEADS + h].astype(jnp.bfloat16)
+                rows = pl.ds((to * HEADS + h) * ROWS, ROWS)
+                stats = jnp.where(lane == h, top[u, rows, :], stats)
+                stats = jnp.where(lane == HEADS + h, tot[u, rows, :], stats)
+                osend[u, to, h] = acc[u, rows, :].astype(jnp.bfloat16)
             ssend[u, to] = stats.T[:8]
             same, o_here_copy, o_there, s_here_copy, s_there = o_copies(u, to)
 
@@ -344,6 +356,39 @@
             def _():
                 o_there.start()
                 s_there.start()
+
+    def attend_chunk(ch, carry):
+        u = ch % 2
+        slots = pl.ds(pl.multiple_of(ch * CHUNK, CHUNK), CHUNK)
+        k_dst = kbuf.at[slots, :, pl.ds(0, HD)]
+        pltpu.make_async_copy(k_dst, k_dst, k_recv.at[ch]).wait()
+        pltpu.make_async_copy(vbuf.at[slots], vbuf.at[slots], v_recv.at[ch]).wait()
+
+        keys = kbuf[slots].reshape(CHUNK * BLK, 2 * HD)
+        values = vbuf[slots].reshape(CHUNK * BLK, HD)
+        scores = lax.dot_general(
+            qaug[u].reshape(2 * HEADS * ROWS, 2 * HD),
+            keys,
+            (((1,), (1,)), ((), ())),
+            preferred_element_type=jnp.float32,
+        )
+        old = top[u]
+        new = jnp.maximum(old, jnp.max(scores, axis=1, keepdims=True))
+        shrink = jnp.exp2((old - new) * LOG2_SCALE)
+        weights = jnp.exp2(scores * LOG2_SCALE - new[:, :1] * LOG2_SCALE)
+        top[u] = new
+        tot[u] = tot[u] * shrink + jnp.sum(weights, axis=1, keepdims=True)
+        acc[u] = acc[u] * shrink + jnp.dot(
+            weights.astype(jnp.bfloat16), values, preferred_element_type=jnp.float32
+        )
+
+        @pl.when(ch >= CHUNKS - 2)
+        def _():
+            send_partials(u)
+
+        return carry
+
+    lax.fori_loop(0, CHUNKS, attend_chunk, 0)
 
     own_copy.wait_send()
     other = 1 - tp % 2
@@ -443,6 +488,8 @@
 
     lax.fori_loop(0, TILES, sum_last, 0)
 
+    for i in range(2):
+        landed((squares_x, squares_y)[i], sq_send.at[i])
     sent = hbuf.at[pl.ds(0, SHARDS - 1)]
     pltpu.make_async_copy(sent, sent, ag_send).wait()
     sent = kbuf.at[pl.ds(0, SLOTS - 2), :, pl.ds(0, HD)]
@@ -479,22 +526,16 @@
     prefix_lengths,
     row_request,
 ):
-    seq = lax.axis_index("seq")
-    table = lax.dynamic_slice_in_dim(block_table, seq * 4, 4, 0)
-    lengths = lax.dynamic_slice_in_dim(prefix_lengths, seq * 4, 4, 0)
-    starts = jnp.arange(64, dtype=jnp.int32)[:, None] * BLK
-    caps = jnp.clip(lengths[None, :] - starts, 0, BLK)
-    table = jnp.pad(table.T, ((0, 0), (0, HD - 4)), constant_values=-1)
-    caps = jnp.pad(caps, ((0, 0), (0, HD - 4)))
     bf16, f32 = jnp.bfloat16, jnp.float32
     vmem = functools.partial(pltpu.VMEM)
     dma = pltpu.SemaphoreType.DMA
     any_spec = pl.BlockSpec(memory_space=pl.ANY)
     vmem_spec = pl.BlockSpec(memory_space=pltpu.VMEM)
+    smem_spec = pl.BlockSpec(memory_space=pltpu.SMEM)
     return pl.pallas_call(
         body,
         out_shape=jax.ShapeDtypeStruct((16, 6144), bf16),
-        in_specs=[any_spec, vmem_spec] + [any_spec] * 5 + [vmem_spec] * 3,
+        in_specs=[any_spec, vmem_spec] + [any_spec] * 5 + [vmem_spec, smem_spec, vmem_spec],
         out_specs=vmem_spec,
         scratch_shapes=[
             vmem((SHARDS, ROWS, FEAT), bf16),
@@ -505,13 +546,20 @@
             vmem((2, 2 * HEADS, ROWS, 2 * HD), bf16),
             vmem((HEADS, ROWS, HD), bf16),
             vmem((2, ROWS, HD), bf16),
-            vmem((2, 2 * HEADS, ROWS, HD), f32),
-            vmem((2, 2 * HEADS, ROWS, HD), f32),
-            vmem((2, 2 * HEADS, ROWS, HD), f32),
+            vmem((2, 2 * HEADS * ROWS, HD), f32),
+            vmem((2, 2 * HEADS * ROWS, HD), f32),
+            vmem((2, 2 * HEADS * ROWS, HD), f32),
             vmem((2, 2, HEADS, ROWS, HD), bf16),
             vmem((2, 2, 8, ROWS), f32),
             vmem((4, HEADS, ROWS, HD), bf16),
             vmem((128, ROWS), f32),
+            vmem((8, ROWS), f32),
+            vmem((3, 8, ROWS), f32),
+            vmem((8, ROWS), f32),
+            vmem((3, 8, ROWS), f32),
+            vmem((HD, HD), jnp.int32),
+            vmem((64, HD), jnp.int32),
+            vmem((64, HD), jnp.int32),
             vmem((ROWS, FEAT), bf16),
             vmem((4, 4, 16, 6144), bf16),
             vmem((3, 4, 16, 3072), bf16),
@@ -521,6 +569,10 @@
             vmem((3, 16, 3072), bf16),
             vmem((3, 16, 3072), bf16),
             dma((4,)),
+            pltpu.SemaphoreType.REGULAR,
+            pltpu.SemaphoreType.REGULAR,
+            dma((2,)),
+            dma((2, 3)),
             dma,
             dma((SHARDS, 2)),
             dma((2,)),
@@ -540,22 +592,22 @@
             dma((2, TILES, 3)),
         ],
         compiler_params=pltpu.CompilerParams(
-            collective_id=0, has_side_effects=True, vmem_limit_bytes=56 << 20
+            collective_id=0, has_side_effects=True, vmem_limit_bytes=60 << 20
         ),
         cost_estimate=pl.CostEstimate(
             flops=10_000_000_000, bytes_accessed=20_000_000, transcendentals=13_000_000
         ),
     )(
         hidden_in,
-        norm_gain.reshape(SHARDS, 1, FEAT),
+        norm_gain.reshape(1, SHARDS * FEAT),
         w_query,
         w_keyval,
         w_out,
         key_pool,
         value_pool,
-        table,
-        caps,
-        row_request.reshape(ROWS, 1),
+        block_table,
+        prefix_lengths,
+        row_request.reshape(1, ROWS),
     )
 
 

time: 174 us -> 142 us (0.82)
  Pallas kernels: 167 us -> 139 us
  local copies, waits for them, and re-layouts: 6.5 us -> 2.94 us
    pallas_call x1, Pallas kernels: 167 us -> 139 us  [per_device(): pl.pallas_call(body, out_shape=jax.ShapeDtypeStruct((16, 6144), bf16), in...]
where the time goes in v2:
time: 142 us
  Pallas kernels  139 us (98%)
  local copies, waits for them, and re-layouts  2.94 us (2%)
    pallas_call x1, Pallas kernels, per_device(): pl.pallas_call(body, out_shape=jax.ShapeDtypeStruct((16, 6144), bf16), in...  139 us

profile of v2, /device:TPU:0, one launch (start us, length us, event | category | flops | bytes accessed | tf_op | source)
XLA Modules:
  0.0 141.9 jit_solution(3703381813756122941)
XLA Ops:
  0.0 1.3 reshape.6.gain
  1.3 139.0 %shard_map.100 = bf16[16,6144]{1,0:T(8,128)(2,1)} custom-call(bf16[256,384]{1,0:T(8,128)(2,1)} %hidden.1, bf16[1,6144]{1,0:T(2,128)(2,1)} %reshape.6.gain, bf16[6144,384]{1,0:T(8,128)(2,1)} %w_query.1, bf16[6144,128]{1,0:T(8,128)(2,1)} %w_keyval.1, bf16[384,6144]{1,0:T(8,128)(2,1)} %w_out.1, bf16[8,128,1024]{2,1,0:T(8,128)(2,1)} %key_pool.1, ...), custom_call_target="tpu_custom_call" | custom-call | flops 10000000000 | bytes 20000000 | tf_op jit(solution)/shard_map/pallas_call | solution.py:535
  140.3 1.6 %copy.12 = bf16[16,6144]{1,0:T(8,128)(2,1)} copy(bf16[16,6144]{1,0:T(8,128)(2,1)} %shard_map.100) | data formatting | bytes 393216

commit v3 on v2

--- a/solution.py
+++ b/solution.py
@@ -17,6 +17,7 @@
 SLOTS = 64
 CHUNK = 8
 CHUNKS = 8
+STAGED = 6
 TILE = 512
 TILES = 6
 MASKED = -1e30
@@ -44,6 +45,8 @@
     wo,
     kbuf,
     vbuf,
+    kstage,
+    vstage,
     qaug,
     qown,
     kvown,
@@ -70,13 +73,15 @@
     fin_a,
     fin_b,
     load_sem,
-    column_sem,
     plane_sem,
     sq_send,
     sq_recv,
     ag_send,
     ag_recv,
     kv_send,
+    leg_send,
+    k_stage,
+    v_stage,
     k_recv,
     v_recv,
     q_send,
@@ -132,8 +137,8 @@
     own_sum = jnp.broadcast_to(jnp.sum(wide * wide, axis=1, keepdims=True), (ROWS, HD))
     squares_own[...] = own_sum.T[:8]
     pl.semaphore_wait(barrier, 13)
-    for d in (1, 3, 2):
-        signal(column_sem, seq, y_peer(d))
+    signal(plane_sem, seq, x_peer(1))
+    signal(plane_sem, seq, x_peer(3))
 
     half = ROWS // 2
     for d in (1, 3, 2):
@@ -144,11 +149,12 @@
         remote(hbuf.at[tp], hbuf.at[tp], ag_send, ag_recv.at[tp, 0], seq, x_peer(d)).start()
         remote(hbuf.at[tp], hbuf.at[tp], ag_send, ag_recv.at[tp, 0], seq, y_peer(d)).start()
 
-    def send_chunk(ch, carry):
-        u = ch % 2
-        ix = ch // 4
-        iy = (ch // 2) % 2
-        slot = ch * CHUNK + seq
+    def place(ch):
+        pair = ch // 2
+        return ch % 2, (pair + 1) // 2 % 2, (pair + 1) % 2
+
+    def send_stage(ch, carry):
+        u, ix, iy = place(ch)
         back = u + ix * (3 - 2 * u)
 
         def send_one(i, c):
@@ -157,37 +163,34 @@
             kx = (x + 4 - turn * back) % 4
             shift = (kx % 2) * turn
             ky = ((y + 4 - shift) % 4 // 2 + iy) % 2
-            xd = (kx + 4 + turn * u) % 4
-            yd = iy * ring_partner(y, shift) + (1 - iy) * y
             lanes = pl.ds(pl.multiple_of((2 * kx + ky) * HD, HD), HD)
-            dest = xd * 4 + yd
-            here = (i == 0) & (dest == tp)
-
-            @pl.when(here)
+            k_src, v_src = key_pool.at[g, :, lanes], value_pool.at[g, :, lanes]
+
+            def send(k_dst, v_dst):
+                @pl.when(i == 0)
+                def _():
+                    pltpu.make_async_copy(k_src, k_dst, k_stage.at[ch]).start()
+                    pltpu.make_async_copy(v_src, v_dst, v_stage.at[ch]).start()
+
+                @pl.when(i != 0)
+                def _():
+                    remote(k_src, k_dst, kv_send.at[0], k_stage.at[ch], g, tp).start()
+                    remote(v_src, v_dst, kv_send.at[1], v_stage.at[ch], g, tp).start()
+
+            @pl.when(ch < STAGED)
             def _():
-                pltpu.make_async_copy(
-                    key_pool.at[g, :, lanes], kbuf.at[slot, :, pl.ds(0, HD)], k_recv.at[ch]
-                ).start()
-                pltpu.make_async_copy(
-                    value_pool.at[g, :, lanes], vbuf.at[slot], v_recv.at[ch]
-                ).start()
-
-            @pl.when(jnp.logical_not(here))
+                send(kstage.at[ch, seq], vstage.at[ch, seq])
+
+            @pl.when(ch >= STAGED)
             def _():
-                remote(
-                    key_pool.at[g, :, lanes], kbuf.at[slot, :, pl.ds(0, HD)],
-                    kv_send.at[0], k_recv.at[ch], g, dest,
-                ).start()
-                remote(
-                    value_pool.at[g, :, lanes], vbuf.at[slot],
-                    kv_send.at[1], v_recv.at[ch], g, dest,
-                ).start()
+                slot = ch * CHUNK + seq
+                send(kbuf.at[slot, :, pl.ds(0, HD)], vbuf.at[slot])
 
             return c
 
         return lax.fori_loop(0, 8, send_one, carry)
 
-    lax.fori_loop(0, 2, send_chunk, 0)
+    lax.fori_loop(0, 4, send_stage, 0)
 
     def landed(ref, sem):
         pltpu.make_async_copy(ref, ref, sem).wait()
@@ -202,9 +205,20 @@
             squares_mid, squares_y.at[d - 1], sq_send.at[1], sq_recv.at[1, d - 1], seq, y_peer(d)
         ).start()
 
-    pl.semaphore_wait(column_sem, 3)
-    signal(plane_sem, seq, x_peer(1))
-    signal(plane_sem, seq, x_peer(3))
+    def send_leg(ch, carry):
+        u, ix, iy = place(ch)
+        kx = (x + 4 - sign * (u + ix * (3 - 2 * u))) % 4
+        shift = (kx % 2) * sign
+        xd = (kx + 4 + sign * u) % 4
+        yd = iy * ring_partner(y, shift) + (1 - iy) * y
+        slots = pl.ds(pl.multiple_of(ch * CHUNK, CHUNK), CHUNK)
+        dest = xd * 4 + yd
+        landed(kstage.at[ch], k_stage.at[ch])
+        landed(vstage.at[ch], v_stage.at[ch])
+        k_dst = kbuf.at[slots, :, pl.ds(0, HD)]
+        remote(kstage.at[ch], k_dst, leg_send.at[0], k_recv.at[ch], seq, dest).start()
+        remote(vstage.at[ch], vbuf.at[slots], leg_send.at[1], v_recv.at[ch], seq, dest).start()
+        return carry
 
     top_rows, low_rows = pl.ds(0, half), pl.ds(half, half)
     for d in (1, 3, 2):
@@ -224,7 +238,6 @@
             ).start()
 
     pl.semaphore_wait(plane_sem, 2)
-    lax.fori_loop(2, CHUNKS, send_chunk, 0)
 
     lane = lax.broadcasted_iota(jnp.int32, (ROWS, HD), 1)
     first_request = seq // 2 * 8
@@ -245,9 +258,7 @@
 
     def mask_slot(slot, carry):
         ch, s = slot // 8, slot % 8
-        u = ch % 2
-        ix = ch // 4
-        iy = (ch // 2) % 2
+        u, ix, iy = place(ch)
         shift = ((x + 4 - sign * u) % 4) % 2 * sign
         xs = (x + 4 + sign * ix * (2 * u - 1)) % 4
         ys = iy * ring_partner(y, shift) + (1 - iy) * y
@@ -261,6 +272,7 @@
     tot[...] = jnp.zeros_like(tot)
     acc[...] = jnp.zeros_like(acc)
 
+    lax.fori_loop(4, 6, send_stage, 0)
     for d in range(3):
         landed(squares_y.at[d], sq_recv.at[1, d])
         square_sums = square_sums + squares_y[d]
@@ -312,6 +324,8 @@
             pl.when(same)(here.start)
             pl.when(jnp.logical_not(same))(there.start)
     own_copy.start()
+    lax.fori_loop(0, 4, send_leg, 0)
+    lax.fori_loop(6, CHUNKS, send_stage, 0)
     for u in range(2):
         for part_half in range(2):
             dst = qaug.at[u, pl.ds(part_half * HEADS, HEADS), :, pl.ds(0, HD)]
@@ -360,9 +374,22 @@
     def attend_chunk(ch, carry):
         u = ch % 2
         slots = pl.ds(pl.multiple_of(ch * CHUNK, CHUNK), CHUNK)
+
+        @pl.when(ch == 1)
+        def _():
+            lax.fori_loop(4, STAGED, send_leg, 0)
+
         k_dst = kbuf.at[slots, :, pl.ds(0, HD)]
-        pltpu.make_async_copy(k_dst, k_dst, k_recv.at[ch]).wait()
-        pltpu.make_async_copy(vbuf.at[slots], vbuf.at[slots], v_recv.at[ch]).wait()
+
+        @pl.when(ch < STAGED)
+        def _():
+            landed(k_dst, k_recv.at[ch])
+            landed(vbuf.at[slots], v_recv.at[ch])
+
+        @pl.when(ch >= STAGED)
+        def _():
+            landed(k_dst, k_stage.at[ch])
+            landed(vbuf.at[slots], v_stage.at[ch])
 
         keys = kbuf[slots].reshape(CHUNK * BLK, 2 * HD)
         values = vbuf[slots].reshape(CHUNK * BLK, HD)
@@ -492,10 +519,9 @@
         landed((squares_x, squares_y)[i], sq_send.at[i])
     sent = hbuf.at[pl.ds(0, SHARDS - 1)]
     pltpu.make_async_copy(sent, sent, ag_send).wait()
-    sent = kbuf.at[pl.ds(0, SLOTS - 2), :, pl.ds(0, HD)]
-    pltpu.make_async_copy(sent, sent, kv_send.at[0]).wait()
-    sent = vbuf.at[pl.ds(0, SLOTS - 2)]
-    pltpu.make_async_copy(sent, sent, kv_send.at[1]).wait()
+    for i in range(2):
+        landed(vbuf.at[pl.ds(0, SLOTS - CHUNKS)], kv_send.at[i])
+        landed(vbuf.at[pl.ds(0, STAGED * CHUNK)], leg_send.at[i])
     for u in range(2):
         for j in range(2):
             same, _, there = q_copies(u, j)
@@ -543,6 +569,8 @@
             vmem((FEAT, 6144), bf16),
             vmem((SLOTS, BLK, 2 * HD), bf16),
             vmem((SLOTS, BLK, HD), bf16),
+            vmem((STAGED, CHUNK, BLK, HD), bf16),
+            vmem((STAGED, CHUNK, BLK, HD), bf16),
             vmem((2, 2 * HEADS, ROWS, 2 * HD), bf16),
             vmem((HEADS, ROWS, HD), bf16),
             vmem((2, ROWS, HD), bf16),
@@ -570,12 +598,14 @@
             vmem((3, 16, 3072), bf16),
             dma((4,)),
             pltpu.SemaphoreType.REGULAR,
-            pltpu.SemaphoreType.REGULAR,
             dma((2,)),
             dma((2, 3)),
             dma,
             dma((SHARDS, 2)),
             dma((2,)),
+            dma((2,)),
+            dma((CHUNKS,)),
+            dma((CHUNKS,)),
             dma((CHUNKS,)),
             dma((CHUNKS,)),
             dma((2, 2)),

time: 142 us -> 133 us (0.937)
  Pallas kernels: 139 us -> 129 us
    pallas_call x1, Pallas kernels: 139 us -> 129 us  [per_device(): pl.pallas_call(body, out_shape=jax.ShapeDtypeStruct((16, 6144), bf16), in...]
where the time goes in v3:
time: 133 us; the launch traced here: 132 us
  Pallas kernels  129 us (97%)
  local copies, waits for them, and re-layouts  2.94 us (2%)
    pallas_call x1, Pallas kernels, per_device(): pl.pallas_call(body, out_shape=jax.ShapeDtypeStruct((16, 6144), bf16), in...  129 us

profile of v3, /device:TPU:0, one launch (start us, length us, event | category | flops | bytes accessed | tf_op | source)
XLA Modules:
  0.0 131.6 jit_solution(15525617419759313220)
XLA Ops:
  0.0 1.3 %reshape.6.gain = bf16[1,6144]{1,0:T(2,128)(2,1)} reshape(bf16[6144]{0:T(1024)(128)(2,1)} %param.11) | data formatting | bytes 24576 | tf_op jit(solution)/shard_map/reshape | solution.py:632
  1.3 128.6 %shard_map.100 = bf16[16,6144]{1,0:T(8,128)(2,1)} custom-call(bf16[256,384]{1,0:T(8,128)(2,1)} %hidden.1, bf16[1,6144]{1,0:T(2,128)(2,1)} %reshape.6.gain, bf16[6144,384]{1,0:T(8,128)(2,1)} %w_query.1, bf16[6144,128]{1,0:T(8,128)(2,1)} %w_keyval.1, bf16[384,6144]{1,0:T(8,128)(2,1)} %w_out.1, bf16[8,128,1024]{2,1,0:T(8,128)(2,1)} %key_pool.1, ...), custom_call_target="tpu_custom_call" | custom-call | flops 10000000000 | bytes 20000000 | tf_op jit(solution)/shard_map/pallas_call | solution.py:561
  130.0 1.6 %copy.12 = bf16[16,6144]{1,0:T(8,128)(2,1)} copy(bf16[16,6144]{1,0:T(8,128)(2,1)} %shard_map.100) | data formatting | bytes 393216

commit v4 on v3

--- a/solution.py
+++ b/solution.py
@@ -151,7 +151,13 @@
 
     def place(ch):
         pair = ch // 2
-        return ch % 2, (pair + 1) // 2 % 2, (pair + 1) % 2
+        return ch % 2, ((pair + 1) // 2 + 1) % 2, pair // 2
+
+    def is_local(ch):
+        return ch // 2 == 1
+
+    def stage(ch):
+        return (ch + 6) % 8 % 6
 
     def send_stage(ch, carry):
         u, ix, iy = place(ch)
@@ -177,11 +183,11 @@
                     remote(k_src, k_dst, kv_send.at[0], k_stage.at[ch], g, tp).start()
                     remote(v_src, v_dst, kv_send.at[1], v_stage.at[ch], g, tp).start()
 
-            @pl.when(ch < STAGED)
+            @pl.when(jnp.logical_not(is_local(ch)))
             def _():
-                send(kstage.at[ch, seq], vstage.at[ch, seq])
-
-            @pl.when(ch >= STAGED)
+                send(kstage.at[stage(ch), seq], vstage.at[stage(ch), seq])
+
+            @pl.when(is_local(ch))
             def _():
                 slot = ch * CHUNK + seq
                 send(kbuf.at[slot, :, pl.ds(0, HD)], vbuf.at[slot])
@@ -213,11 +219,11 @@
         yd = iy * ring_partner(y, shift) + (1 - iy) * y
         slots = pl.ds(pl.multiple_of(ch * CHUNK, CHUNK), CHUNK)
         dest = xd * 4 + yd
-        landed(kstage.at[ch], k_stage.at[ch])
-        landed(vstage.at[ch], v_stage.at[ch])
+        landed(kstage.at[stage(ch)], k_stage.at[ch])
+        landed(vstage.at[stage(ch)], v_stage.at[ch])
         k_dst = kbuf.at[slots, :, pl.ds(0, HD)]
-        remote(kstage.at[ch], k_dst, leg_send.at[0], k_recv.at[ch], seq, dest).start()
-        remote(vstage.at[ch], vbuf.at[slots], leg_send.at[1], v_recv.at[ch], seq, dest).start()
+        remote(kstage.at[stage(ch)], k_dst, leg_send.at[0], k_recv.at[ch], seq, dest).start()
+        remote(vstage.at[stage(ch)], vbuf.at[slots], leg_send.at[1], v_recv.at[ch], seq, dest).start()
         return carry
 
     top_rows, low_rows = pl.ds(0, half), pl.ds(half, half)
@@ -324,12 +330,14 @@
             pl.when(same)(here.start)
             pl.when(jnp.logical_not(same))(there.start)
     own_copy.start()
-    lax.fori_loop(0, 4, send_leg, 0)
+    lax.fori_loop(0, 2, send_leg, 0)
     lax.fori_loop(6, CHUNKS, send_stage, 0)
     for u in range(2):
         for part_half in range(2):
             dst = qaug.at[u, pl.ds(part_half * HEADS, HEADS), :, pl.ds(0, HD)]
             pltpu.make_async_copy(dst, dst, q_recv.at[u, part_half]).wait()
+
+    lax.fori_loop(4, 6, send_leg, 0)
 
     def o_copies(u, to):
         kx = (x + 4 - sign * u) % 4
@@ -375,18 +383,18 @@
         u = ch % 2
         slots = pl.ds(pl.multiple_of(ch * CHUNK, CHUNK), CHUNK)
 
-        @pl.when(ch == 1)
+        @pl.when((ch == 2) | (ch == 3))
         def _():
-            lax.fori_loop(4, STAGED, send_leg, 0)
+            send_leg(ch + 4, 0)
 
         k_dst = kbuf.at[slots, :, pl.ds(0, HD)]
 
-        @pl.when(ch < STAGED)
+        @pl.when(jnp.logical_not(is_local(ch)))
         def _():
             landed(k_dst, k_recv.at[ch])
             landed(vbuf.at[slots], v_recv.at[ch])
 
-        @pl.when(ch >= STAGED)
+        @pl.when(is_local(ch))
         def _():
             landed(k_dst, k_stage.at[ch])
             landed(vbuf.at[slots], v_stage.at[ch])

time: 133 us -> 119 us (0.89)
  Pallas kernels: 129 us -> 116 us
    pallas_call x1, Pallas kernels: 129 us -> 116 us  [per_device(): pl.pallas_call(body, out_shape=jax.ShapeDtypeStruct((16, 6144), bf16), in...]
where the time goes in v4:
time: 119 us
  Pallas kernels  116 us (97%)
  local copies, waits for them, and re-layouts  2.94 us (2%)
    pallas_call x1, Pallas kernels, per_device(): pl.pallas_call(body, out_shape=jax.ShapeDtypeStruct((16, 6144), bf16), in...  116 us

profile of v4, /device:TPU:0, one launch (start us, length us, event | category | flops | bytes accessed | tf_op | source)
XLA Modules:
  0.0 118.7 jit_solution(1671660644622903536)
XLA Ops:
  0.0 1.3 %reshape.6.gain = bf16[1,6144]{1,0:T(2,128)(2,1)} reshape(bf16[6144]{0:T(1024)(128)(2,1)} %param.11) | data formatting | bytes 24576 | tf_op jit(solution)/shard_map/reshape | solution.py:640
  1.3 115.8 %shard_map.100 = bf16[16,6144]{1,0:T(8,128)(2,1)} custom-call(bf16[256,384]{1,0:T(8,128)(2,1)} %hidden.1, bf16[1,6144]{1,0:T(2,128)(2,1)} %reshape.6.gain, bf16[6144,384]{1,0:T(8,128)(2,1)} %w_query.1, bf16[6144,128]{1,0:T(8,128)(2,1)} %w_keyval.1, bf16[384,6144]{1,0:T(8,128)(2,1)} %w_out.1, bf16[8,128,1024]{2,1,0:T(8,128)(2,1)} %key_pool.1, ...), custom_call_target="tpu_custom_call" | custom-call | flops 10000000000 | bytes 20000000 | tf_op jit(solution)/shard_map/pallas_call | solution.py:569
  117.1 1.6 %copy.12 = bf16[16,6144]{1,0:T(8,128)(2,1)} copy(bf16[16,6144]{1,0:T(8,128)(2,1)} %shard_map.100) | data formatting | bytes 393216

commit v5 on v4

--- a/solution.py
+++ b/solution.py
@@ -68,6 +68,8 @@
     part,
     rs_a,
     rs_b,
+    via_a,
+    via_b,
     mid_a,
     mid_b,
     fin_a,
@@ -92,6 +94,8 @@
     o_recv,
     s_send,
     s_recv,
+    via_send,
+    via_recv,
     rs1_send,
     rs1_recv,
     rs2_send,
@@ -140,14 +144,18 @@
     signal(plane_sem, seq, x_peer(1))
     signal(plane_sem, seq, x_peer(3))
 
-    half = ROWS // 2
+    half, quarter = ROWS // 2, ROWS // 4
     for d in (1, 3, 2):
         remote(
             squares_own, squares_x.at[d - 1], sq_send.at[0], sq_recv.at[0, d - 1], seq, x_peer(d)
         ).start()
-    for d in (1, 3, 2):
-        remote(hbuf.at[tp], hbuf.at[tp], ag_send, ag_recv.at[tp, 0], seq, x_peer(d)).start()
-        remote(hbuf.at[tp], hbuf.at[tp], ag_send, ag_recv.at[tp, 0], seq, y_peer(d)).start()
+    def forward(shard, first, rows, index, t):
+        block = hbuf.at[shard, pl.ds(first, rows)]
+        remote(block, block, ag_send, ag_recv.at[shard, index], seq, t).start()
+
+    for d in (1, 3):
+        forward(tp, 0, ROWS, 0, x_peer(d))
+        forward(tp, 0, ROWS, 0, y_peer(d))
 
     def place(ch):
         pair = ch // 2
@@ -226,25 +234,101 @@
         remote(vstage.at[stage(ch)], vbuf.at[slots], leg_send.at[1], v_recv.at[ch], seq, dest).start()
         return carry
 
-    top_rows, low_rows = pl.ds(0, half), pl.ds(half, half)
-    for d in (1, 3, 2):
-        from_x = x_peer(4 - d)
-        landed(hbuf.at[from_x], ag_recv.at[from_x, 0])
-        for e in (1, 3, 2):
-            remote(
-                hbuf.at[from_x, top_rows], hbuf.at[from_x, top_rows],
-                ag_send, ag_recv.at[from_x, 0], seq, y_peer(e),
-            ).start()
-        from_y = y_peer(4 - d)
-        landed(hbuf.at[from_y], ag_recv.at[from_y, 0])
-        for e in (1, 3, 2):
-            remote(
-                hbuf.at[from_y, low_rows], hbuf.at[from_y, low_rows],
-                ag_send, ag_recv.at[from_y, 1], seq, x_peer(e),
-            ).start()
+    def arrived(shard, first, rows, index):
+        landed(hbuf.at[shard, pl.ds(first, rows)], ag_recv.at[shard, index])
+
+    for d in (3, 1):
+        shard = x_peer(d)
+        arrived(shard, 0, ROWS, 0)
+        forward(shard, 0 if d == 3 else half, half, 0 if d == 3 else 1, x_peer(4 - d))
+        forward(shard, 0, half, 0, y_peer(1))
+        forward(shard, 0, half, 0, y_peer(3))
+        shard = y_peer(d)
+        arrived(shard, 0, ROWS, 0)
+        forward(shard, half if d == 3 else 0, half, 1 if d == 3 else 0, y_peer(4 - d))
+        forward(shard, half, half, 2, x_peer(1))
+        forward(shard, half, half, 2, x_peer(3))
+    shard = x_peer(2)
+    arrived(shard, 0, half, 0)
+    forward(shard, 0, half, 0, y_peer(1))
+    forward(shard, 0, half, 0, y_peer(3))
+    shard = y_peer(2)
+    arrived(shard, half, half, 1)
+    forward(shard, half, half, 2, x_peer(1))
+    forward(shard, half, half, 2, x_peer(3))
+    for e in (3, 1, 2):
+        for d in (3, 1):
+            shard = (x + e) % 4 * 4 + (y + d) % 4
+            arrived(shard, 0, half, 0)
+            forward(shard, 0 if d == 3 else quarter, quarter, 0 if d == 3 else 1, y_peer(4 - d))
+            shard = (x + d) % 4 * 4 + (y + e) % 4
+            arrived(shard, half, half, 2)
+            forward(
+                shard, half if d == 3 else half + quarter, quarter, 2 if d == 3 else 3, x_peer(4 - d)
+            )
 
     pl.semaphore_wait(plane_sem, 2)
 
+    lax.fori_loop(4, 6, send_stage, 0)
+    for d in range(3):
+        landed(squares_y.at[d], sq_recv.at[1, d])
+        square_sums = square_sums + squares_y[d]
+    square_cols = jnp.broadcast_to(square_sums[:1], (HD, ROWS)).T
+    factor = lax.rsqrt(square_cols[:, :1] / (SHARDS * FEAT) + 1e-5)
+    loads[0].wait()
+    loads[1].wait()
+
+    def project(t, total):
+        feats = pl.ds(pl.multiple_of(t * FEAT, FEAT), FEAT)
+        normed = (
+            hbuf[t].astype(jnp.float32) * factor * gain[:, feats].astype(jnp.float32)
+        ).astype(jnp.bfloat16)
+        return total + jnp.dot(normed, wqkv[feats, :], preferred_element_type=jnp.float32)
+
+    def project_line(i, total):
+        along = i // 4
+        d = i % 4
+        return project((x + (1 - along) * d) % 4 * 4 + (y + along * d) % 4, total)
+
+    def project_far(i, total):
+        return project((x + 1 + i // 3) % 4 * 4 + (y + 1 + i % 3) % 4, total)
+
+    arrived(x_peer(2), half, half, 1)
+    arrived(y_peer(2), 0, half, 0)
+    projected = lax.fori_loop(0, 4, project_line, jnp.zeros((ROWS, 512), jnp.float32))
+    projected = lax.fori_loop(5, 8, project_line, projected)
+    for e in (3, 1, 2):
+        shard = (x + e) % 4 * 4 + (y + 2) % 4
+        arrived(shard, 0, quarter, 0)
+        arrived(shard, quarter, quarter, 1)
+        shard = (x + 2) % 4 * 4 + (y + e) % 4
+        arrived(shard, half, quarter, 2)
+        arrived(shard, half + quarter, quarter, 3)
+    projected = lax.fori_loop(0, 9, project_far, projected).astype(jnp.bfloat16)
+    for h in range(HEADS):
+        qown[h] = projected[:, h * HD : (h + 1) * HD]
+    kvown[tp % 2] = projected[:, HEADS * HD :]
+
+    own_copy = remote(
+        kvown.at[tp % 2], kvown.at[tp % 2], own_send, own_recv.at[tp % 2], seq, tp + 1 - 2 * (tp % 2)
+    )
+    own_half = tp % 2
+
+    def q_copies(u, j):
+        t = (x + 4 + sign * u) % 4 * 4 + (y // 2 * 2 + j + 4 + x % 2 * sign) % 4
+        dst = qaug.at[u, pl.ds(own_half * HEADS, HEADS), :, pl.ds(0, HD)]
+        there = remote(qown, dst, q_send.at[u, j], q_recv.at[u, own_half], seq, t)
+        here = pltpu.make_async_copy(qown, dst, q_recv.at[u, own_half])
+        return t == tp, here, there
+
+    for u in range(2):
+        for j in range(2):
+            same, here, there = q_copies(u, j)
+            pl.when(same)(here.start)
+            pl.when(jnp.logical_not(same))(there.start)
+    own_copy.start()
+    lax.fori_loop(0, 2, send_leg, 0)
+    lax.fori_loop(6, CHUNKS, send_stage, 0)
     lane = lax.broadcasted_iota(jnp.int32, (ROWS, HD), 1)
     first_request = seq // 2 * 8
     requests = jnp.broadcast_to(row_req[...], (HD, ROWS)).T
@@ -278,60 +362,6 @@
     tot[...] = jnp.zeros_like(tot)
     acc[...] = jnp.zeros_like(acc)
 
-    lax.fori_loop(4, 6, send_stage, 0)
-    for d in range(3):
-        landed(squares_y.at[d], sq_recv.at[1, d])
-        square_sums = square_sums + squares_y[d]
-    square_cols = jnp.broadcast_to(square_sums[:1], (HD, ROWS)).T
-    factor = lax.rsqrt(square_cols[:, :1] / (SHARDS * FEAT) + 1e-5)
-    loads[0].wait()
-    loads[1].wait()
-
-    def project(t, total):
-        feats = pl.ds(pl.multiple_of(t * FEAT, FEAT), FEAT)
-        normed = (
-            hbuf[t].astype(jnp.float32) * factor * gain[:, feats].astype(jnp.float32)
-        ).astype(jnp.bfloat16)
-        return total + jnp.dot(normed, wqkv[feats, :], preferred_element_type=jnp.float32)
-
-    def project_line(i, total):
-        along = i // 4
-        d = i % 4
-        return project((x + (1 - along) * d) % 4 * 4 + (y + along * d) % 4, total)
-
-    def project_far(i, total):
-        shard = (x + 1 + i // 3) % 4 * 4 + (y + 1 + i % 3) % 4
-        landed(hbuf.at[shard, top_rows], ag_recv.at[shard, 0])
-        landed(hbuf.at[shard, low_rows], ag_recv.at[shard, 1])
-        return project(shard, total)
-
-    projected = lax.fori_loop(0, 4, project_line, jnp.zeros((ROWS, 512), jnp.float32))
-    projected = lax.fori_loop(5, 8, project_line, projected)
-    projected = lax.fori_loop(0, 9, project_far, projected).astype(jnp.bfloat16)
-    for h in range(HEADS):
-        qown[h] = projected[:, h * HD : (h + 1) * HD]
-    kvown[tp % 2] = projected[:, HEADS * HD :]
-
-    own_copy = remote(
-        kvown.at[tp % 2], kvown.at[tp % 2], own_send, own_recv.at[tp % 2], seq, tp + 1 - 2 * (tp % 2)
-    )
-    own_half = tp % 2
-
-    def q_copies(u, j):
-        t = (x + 4 + sign * u) % 4 * 4 + (y // 2 * 2 + j + 4 + x % 2 * sign) % 4
-        dst = qaug.at[u, pl.ds(own_half * HEADS, HEADS), :, pl.ds(0, HD)]
-        there = remote(qown, dst, q_send.at[u, j], q_recv.at[u, own_half], seq, t)
-        here = pltpu.make_async_copy(qown, dst, q_recv.at[u, own_half])
-        return t == tp, here, there
-
-    for u in range(2):
-        for j in range(2):
-            same, here, there = q_copies(u, j)
-            pl.when(same)(here.start)
-            pl.when(jnp.logical_not(same))(there.start)
-    own_copy.start()
-    lax.fori_loop(0, 2, send_leg, 0)
-    lax.fori_loop(6, CHUNKS, send_stage, 0)
     for u in range(2):
         for part_half in range(2):
             dst = qaug.at[u, pl.ds(part_half * HEADS, HEADS), :, pl.ds(0, HD)]
@@ -454,8 +484,22 @@
 
     loads[2].wait()
 
-    def columns(tile, first=0):
-        return pl.ds(pl.multiple_of(first + tile * TILE, TILE), TILE)
+    def columns(tile, first=0, width=TILE):
+        return pl.ds(pl.multiple_of(first + tile * TILE, TILE // 2), width)
+
+    def half_columns(tile):
+        return pl.ds(pl.multiple_of(tile * (TILE // 2), TILE // 2), TILE // 2)
+
+    def first(side):
+        return side * TILES * TILE
+
+    def ring_peer(side, d):
+        return (x_peer, y_peer)[side](d)
+
+    def ring_block(side, d, cols):
+        if side == 0:
+            return part.at[(x + d) % 4, :, :, cols]
+        return part.at[:, (y + d) % 4, :, cols]
 
     def project_out(tile, carry):
         for side in range(2):
@@ -465,33 +509,47 @@
                 .astype(jnp.bfloat16)
                 .reshape(4, 4, 16, TILE)
             )
-            for d in (1, 3, 2):
-                if side == 0:
-                    src, t = part.at[(x + d) % 4, :, :, cols], (x + d) % 4 * 4 + y
-                else:
-                    src, t = part.at[:, (y + d) % 4, :, cols], x * 4 + (y + d) % 4
-                dst = (rs_a, rs_b)[side].at[d - 1, :, :, columns(tile)]
+            for d in (1, 3):
+                src = ring_block(side, 2, columns(tile, first(side) + (TILE // 2 if d == 3 else 0), TILE // 2))
+                dst = (via_a, via_b)[side].at[d // 2, :, :, half_columns(tile)]
                 remote(
-                    src, dst, rs1_send.at[side], rs1_recv.at[side, tile, d - 1], seq, t
+                    src, dst, via_send.at[side], via_recv.at[side, tile, d // 2], seq, ring_peer(side, d)
                 ).start()
         return carry
 
     lax.fori_loop(0, TILES, project_out, 0)
 
+    def relay(tile, carry):
+        for side in range(2):
+            via = (via_a, via_b)[side]
+            for d in (1, 3):
+                passing = via.at[d // 2, :, :, half_columns(tile)]
+                landed(passing, via_recv.at[side, tile, d // 2])
+                block = ring_block(
+                    side, d, columns(tile, first(side) + (TILE // 2 if d == 3 else 0), TILE // 2)
+                )
+                block[...] = (
+                    block[...].astype(jnp.float32) + passing[...].astype(jnp.float32)
+                ).astype(jnp.bfloat16)
+                remote(
+                    ring_block(side, d, columns(tile, first(side))),
+                    (rs_a, rs_b)[side].at[d // 2, :, :, columns(tile)],
+                    rs1_send.at[side], rs1_recv.at[side, tile, d // 2], seq, ring_peer(side, d),
+                ).start()
+        return carry
+
+    lax.fori_loop(0, TILES, relay, 0)
+
     def sum_first(tile, carry):
         for side in range(2):
-            cols = columns(tile, side * TILES * TILE)
             here = columns(tile)
-            landed = (rs_a, rs_b)[side]
+            arriving = (rs_a, rs_b)[side]
             mid = (mid_a, mid_b)[side]
-            if side == 0:
-                total = part[x, :, :, cols].astype(jnp.float32)
-            else:
-                total = part[:, y, :, cols].astype(jnp.float32)
-            for d in range(3):
-                dst = landed.at[d, :, :, here]
-                pltpu.make_async_copy(dst, dst, rs1_recv.at[side, tile, d]).wait()
-                total = total + landed[d, :, :, here].astype(jnp.float32)
+            total = ring_block(side, 0, columns(tile, first(side)))[...].astype(jnp.float32)
+            for d in range(2):
+                dst = arriving.at[d, :, :, here]
+                landed(dst, rs1_recv.at[side, tile, d])
+                total = total + dst[...].astype(jnp.float32)
             mid[:, :, here] = total.astype(jnp.bfloat16)
             for d in (1, 3, 2):
                 if side == 0:
@@ -509,15 +567,15 @@
     def sum_last(tile, carry):
         for side in range(2):
             here = columns(tile)
-            landed = (fin_a, fin_b)[side]
+            arriving = (fin_a, fin_b)[side]
             if side == 0:
                 total = mid_a[y, :, here].astype(jnp.float32)
             else:
                 total = mid_b[x, :, here].astype(jnp.float32)
             for d in range(3):
-                dst = landed.at[d, :, here]
+                dst = arriving.at[d, :, here]
                 pltpu.make_async_copy(dst, dst, rs2_recv.at[side, tile, d]).wait()
-                total = total + landed[d, :, here].astype(jnp.float32)
+                total = total + arriving[d, :, here].astype(jnp.float32)
             out[:, columns(tile, side * TILES * TILE)] = total.astype(jnp.bfloat16)
         return carry
 
@@ -542,6 +600,7 @@
                 s_there.wait_send()
 
     for side in range(2):
+        landed((via_a, via_b)[side], via_send.at[side])
         sent = (rs_a, rs_b)[side]
         pltpu.make_async_copy(sent, sent, rs1_send.at[side]).wait()
         sent = (fin_a, fin_b)[side]
@@ -598,8 +657,10 @@
             vmem((64, HD), jnp.int32),
             vmem((ROWS, FEAT), bf16),
             vmem((4, 4, 16, 6144), bf16),
-            vmem((3, 4, 16, 3072), bf16),
-            vmem((3, 4, 16, 3072), bf16),
+            vmem((2, 4, 16, 3072), bf16),
+            vmem((2, 4, 16, 3072), bf16),
+            vmem((2, 4, 16, 1536), bf16),
+            vmem((2, 4, 16, 1536), bf16),
             vmem((4, 16, 3072), bf16),
             vmem((4, 16, 3072), bf16),
             vmem((3, 16, 3072), bf16),
@@ -609,7 +670,7 @@
             dma((2,)),
             dma((2, 3)),
             dma,
-            dma((SHARDS, 2)),
+            dma((SHARDS, 4)),
             dma((2,)),
             dma((2,)),
             dma((CHUNKS,)),
@@ -625,7 +686,9 @@
             dma((2, 2)),
             dma((4,)),
             dma((2,)),
-            dma((2, TILES, 3)),
+            dma((2, TILES, 2)),
+            dma((2,)),
+            dma((2, TILES, 2)),
             dma((2,)),
             dma((2, TILES, 3)),
         ],

time: 119 us -> 115 us (0.966)
  Pallas kernels: 116 us -> 112 us
    pallas_call x1, Pallas kernels: 116 us -> 112 us  [per_device(): pl.pallas_call(body, out_shape=jax.ShapeDtypeStruct((16, 6144), bf16), in...]
where the time goes in v5:
time: 115 us
  Pallas kernels  112 us (97%)
  local copies, waits for them, and re-layouts  2.94 us (3%)
    pallas_call x1, Pallas kernels, per_device(): pl.pallas_call(body, out_shape=jax.ShapeDtypeStruct((16, 6144), bf16), in...  112 us

profile of v5, /device:TPU:0, one launch (start us, length us, event | category | flops | bytes accessed | tf_op | source)
XLA Modules:
  0.0 115.2 jit_solution(13096850307516682783)
XLA Ops:
  0.0 1.3 %reshape.6.gain = bf16[1,6144]{1,0:T(2,128)(2,1)} reshape(bf16[6144]{0:T(1024)(128)(2,1)} %param.11) | data formatting | bytes 24576 | tf_op jit(solution)/shard_map/reshape | solution.py:703
  1.3 112.3 %shard_map.100 = bf16[16,6144]{1,0:T(8,128)(2,1)} custom-call(bf16[256,384]{1,0:T(8,128)(2,1)} %hidden.1, bf16[1,6144]{1,0:T(2,128)(2,1)} %reshape.6.gain, bf16[6144,384]{1,0:T(8,128)(2,1)} %w_query.1, bf16[6144,128]{1,0:T(8,128)(2,1)} %w_keyval.1, bf16[384,6144]{1,0:T(8,128)(2,1)} %w_out.1, bf16[8,128,1024]{2,1,0:T(8,128)(2,1)} %key_pool.1, ...), custom_call_target="tpu_custom_call" | custom-call | flops 10000000000 | bytes 20000000 | tf_op jit(solution)/shard_map/pallas_call | solution.py:628
  113.6 1.6 %copy.12 = bf16[16,6144]{1,0:T(8,128)(2,1)} copy(bf16[16,6144]{1,0:T(8,128)(2,1)} %shard_map.100) | data formatting | bytes 393216

commit v6 on v5

--- a/solution.py
+++ b/solution.py
@@ -154,8 +154,11 @@
         remote(block, block, ag_send, ag_recv.at[shard, index], seq, t).start()
 
     for d in (1, 3):
-        forward(tp, 0, ROWS, 0, x_peer(d))
-        forward(tp, 0, ROWS, 0, y_peer(d))
+        forward(tp, 0, half, 0, x_peer(d))
+        forward(tp, half, half, 1, y_peer(d))
+    for d in (1, 3):
+        forward(tp, half, half, 1, x_peer(d))
+        forward(tp, 0, half, 0, y_peer(d))
 
     def place(ch):
         pair = ch // 2
@@ -239,15 +242,23 @@
 
     for d in (3, 1):
         shard = x_peer(d)
-        arrived(shard, 0, ROWS, 0)
-        forward(shard, 0 if d == 3 else half, half, 0 if d == 3 else 1, x_peer(4 - d))
+        arrived(shard, 0, half, 0)
         forward(shard, 0, half, 0, y_peer(1))
         forward(shard, 0, half, 0, y_peer(3))
+        if d == 3:
+            forward(shard, 0, half, 0, x_peer(1))
         shard = y_peer(d)
-        arrived(shard, 0, ROWS, 0)
-        forward(shard, half if d == 3 else 0, half, 1 if d == 3 else 0, y_peer(4 - d))
+        arrived(shard, half, half, 1)
         forward(shard, half, half, 2, x_peer(1))
         forward(shard, half, half, 2, x_peer(3))
+        if d == 3:
+            forward(shard, half, half, 1, y_peer(1))
+    for d in (1, 3):
+        arrived(x_peer(d), half, half, 1)
+        arrived(y_peer(d), 0, half, 0)
+        if d == 1:
+            forward(x_peer(d), half, half, 1, x_peer(3))
+            forward(y_peer(d), 0, half, 0, y_peer(3))
     shard = x_peer(2)
     arrived(shard, 0, half, 0)
     forward(shard, 0, half, 0, y_peer(1))

time: 115 us -> 114 us (level)
  Pallas kernels: 112 us -> 110 us
    pallas_call x1, Pallas kernels: 112 us -> 110 us  [per_device(): pl.pallas_call(body, out_shape=jax.ShapeDtypeStruct((16, 6144), bf16), in...]
where the time goes in v6:
time: 114 us; the launch traced here: 113 us
  Pallas kernels  110 us (96%)
  local copies, waits for them, and re-layouts  2.94 us (3%)
    pallas_call x1, Pallas kernels, per_device(): pl.pallas_call(body, out_shape=jax.ShapeDtypeStruct((16, 6144), bf16), in...  110 us

profile of v6, /device:TPU:0, one launch (start us, length us, event | category | flops | bytes accessed | tf_op | source)
XLA Modules:
  0.0 113.3 jit_solution(11051547669176303844)
XLA Ops:
  0.0 1.3 %reshape.6.gain = bf16[1,6144]{1,0:T(2,128)(2,1)} reshape(bf16[6144]{0:T(1024)(128)(2,1)} %param.11) | data formatting | bytes 24576 | tf_op jit(solution)/shard_map/reshape | solution.py:714
  1.3 110.3 %shard_map.100 = bf16[16,6144]{1,0:T(8,128)(2,1)} custom-call(bf16[256,384]{1,0:T(8,128)(2,1)} %hidden.1, bf16[1,6144]{1,0:T(2,128)(2,1)} %reshape.6.gain, bf16[6144,384]{1,0:T(8,128)(2,1)} %w_query.1, bf16[6144,128]{1,0:T(8,128)(2,1)} %w_keyval.1, bf16[384,6144]{1,0:T(8,128)(2,1)} %w_out.1, bf16[8,128,1024]{2,1,0:T(8,128)(2,1)} %key_pool.1, ...), custom_call_target="tpu_custom_call" | custom-call | flops 10000000000 | bytes 20000000 | tf_op jit(solution)/shard_map/pallas_call | solution.py:639
  111.7 1.6 %copy.12 = bf16[16,6144]{1,0:T(8,128)(2,1)} copy(bf16[16,6144]{1,0:T(8,128)(2,1)} %shard_map.100) | data formatting | bytes 393216

commit v7 on v6

--- a/solution.py
+++ b/solution.py
@@ -338,7 +338,6 @@
             pl.when(same)(here.start)
             pl.when(jnp.logical_not(same))(there.start)
     own_copy.start()
-    lax.fori_loop(0, 2, send_leg, 0)
     lax.fori_loop(6, CHUNKS, send_stage, 0)
     lane = lax.broadcasted_iota(jnp.int32, (ROWS, HD), 1)
     first_request = seq // 2 * 8
@@ -378,6 +377,7 @@
             dst = qaug.at[u, pl.ds(part_half * HEADS, HEADS), :, pl.ds(0, HD)]
             pltpu.make_async_copy(dst, dst, q_recv.at[u, part_half]).wait()
 
+    lax.fori_loop(0, 2, send_leg, 0)
     lax.fori_loop(4, 6, send_leg, 0)
 
     def o_copies(u, to):
@@ -388,7 +388,7 @@
         index = u * 2 + yy % 2
         o_src, o_dst = osend.at[u, to], orecv.at[index]
         s_src = ssend.at[u, to]
-        s_dst = srecv.at[pl.ds(pl.multiple_of(index * 8, 8), 8)]
+        s_dst = srecv.at[u, pl.ds(pl.multiple_of(yy % 2 * 8, 8), 8)]
         return (
             t == tp,
             pltpu.make_async_copy(o_src, o_dst, o_recv.at[index]),
@@ -397,36 +397,37 @@
             remote(s_src, s_dst, s_send.at[u, to], s_recv.at[index], seq, t),
         )
 
-    srecv[pl.ds(32, 96), :] = jnp.zeros((96, ROWS), jnp.float32)
-
-    def send_partials(u):
-        for to in range(2):
-            stats = jnp.zeros((ROWS, HD), jnp.float32)
-            for h in range(HEADS):
-                rows = pl.ds((to * HEADS + h) * ROWS, ROWS)
-                stats = jnp.where(lane == h, top[u, rows, :], stats)
-                stats = jnp.where(lane == HEADS + h, tot[u, rows, :], stats)
-                osend[u, to, h] = acc[u, rows, :].astype(jnp.bfloat16)
-            ssend[u, to] = stats.T[:8]
-            same, o_here_copy, o_there, s_here_copy, s_there = o_copies(u, to)
-
-            @pl.when(same)
-            def _():
-                o_here_copy.start()
-                s_here_copy.start()
-
-            @pl.when(jnp.logical_not(same))
-            def _():
-                o_there.start()
-                s_there.start()
-
-    def attend_chunk(ch, carry):
+    srecv[:, pl.ds(16, 112), :] = jnp.zeros((2, 112, ROWS), jnp.float32)
+
+    def send_partials(u, to):
+        stats = jnp.zeros((ROWS, HD), jnp.float32)
+        for h in range(HEADS):
+            rows = pl.ds(pl.multiple_of((to * HEADS + h) * ROWS, ROWS), ROWS)
+            stats = jnp.where(lane == h, top[u, rows, :], stats)
+            stats = jnp.where(lane == HEADS + h, tot[u, rows, :], stats)
+            osend[u, to, h] = acc[u, rows, :].astype(jnp.bfloat16)
+        ssend[u, to] = stats.T[:8]
+        same, o_here_copy, o_there, s_here_copy, s_there = o_copies(u, to)
+
+        @pl.when(same)
+        def _():
+            o_here_copy.start()
+            s_here_copy.start()
+
+        @pl.when(jnp.logical_not(same))
+        def _():
+            o_there.start()
+            s_there.start()
+
+    def attend_chunk(i, carry):
+        late = i // 4
+        ch = (1 - late) * ((i + 2) % 4) + late * i
         u = ch % 2
         slots = pl.ds(pl.multiple_of(ch * CHUNK, CHUNK), CHUNK)
 
-        @pl.when((ch == 2) | (ch == 3))
+        @pl.when((i == 3) | (i == 4))
         def _():
-            send_leg(ch + 4, 0)
+            send_leg(i + 3, 0)
 
         k_dst = kbuf.at[slots, :, pl.ds(0, HD)]
 
@@ -442,25 +443,37 @@
 
         keys = kbuf[slots].reshape(CHUNK * BLK, 2 * HD)
         values = vbuf[slots].reshape(CHUNK * BLK, HD)
-        scores = lax.dot_general(
-            qaug[u].reshape(2 * HEADS * ROWS, 2 * HD),
-            keys,
-            (((1,), (1,)), ((), ())),
-            preferred_element_type=jnp.float32,
-        )
-        old = top[u]
-        new = jnp.maximum(old, jnp.max(scores, axis=1, keepdims=True))
-        shrink = jnp.exp2((old - new) * LOG2_SCALE)
-        weights = jnp.exp2(scores * LOG2_SCALE - new[:, :1] * LOG2_SCALE)
-        top[u] = new
-        tot[u] = tot[u] * shrink + jnp.sum(weights, axis=1, keepdims=True)
-        acc[u] = acc[u] * shrink + jnp.dot(
-            weights.astype(jnp.bfloat16), values, preferred_element_type=jnp.float32
-        )
+
+        def attend(first_head, heads):
+            rows = pl.ds(pl.multiple_of(first_head * ROWS, ROWS), heads * ROWS)
+            scores = lax.dot_general(
+                qaug[u, pl.ds(first_head, heads)].reshape(heads * ROWS, 2 * HD),
+                keys,
+                (((1,), (1,)), ((), ())),
+                preferred_element_type=jnp.float32,
+            )
+            old = top[u, rows, :]
+            new = jnp.maximum(old, jnp.max(scores, axis=1, keepdims=True))
+            shrink = jnp.exp2((old - new) * LOG2_SCALE)
+            weights = jnp.exp2(scores * LOG2_SCALE - new[:, :1] * LOG2_SCALE)
+            top[u, rows, :] = new
+            tot[u, rows, :] = tot[u, rows, :] * shrink + jnp.sum(weights, axis=1, keepdims=True)
+            acc[u, rows, :] = acc[u, rows, :] * shrink + jnp.dot(
+                weights.astype(jnp.bfloat16), values, preferred_element_type=jnp.float32
+            )
+
+        @pl.when(ch < CHUNKS - 2)
+        def _():
+            attend(0, 2 * HEADS)
 
         @pl.when(ch >= CHUNKS - 2)
         def _():
-            send_partials(u)
+            def attend_owner(to, c):
+                attend(to * HEADS, HEADS)
+                send_partials(u, to)
+                return c
+
+            lax.fori_loop(0, 2, attend_owner, 0)
 
         return carry
 
@@ -474,24 +487,32 @@
     self_scores = [
         jnp.sum(qown[h].astype(jnp.float32) * own_key, axis=1, keepdims=True) for h in range(HEADS)
     ]
-    for i in range(4):
-        pltpu.make_async_copy(orecv.at[i], orecv.at[i], o_recv.at[i]).wait()
-        s_dst = srecv.at[pl.ds(i * 8, 8)]
-        pltpu.make_async_copy(s_dst, s_dst, s_recv.at[i]).wait()
-    stats = srecv[...].T
+    bests = list(self_scores)
+    totals = [jnp.ones((ROWS, 1), jnp.float32)] * HEADS
+    numers = [None] * HEADS
+    for u in range(2):
+        for j in range(2):
+            landed(orecv.at[2 * u + j], o_recv.at[2 * u + j])
+            landed(srecv.at[u, pl.ds(j * 8, 8)], s_recv.at[2 * u + j])
+        stats = srecv[u].T
+        for h in range(HEADS):
+            tops = [stats[:, j * 8 + h : j * 8 + h + 1] for j in range(2)]
+            best = jnp.maximum(jnp.maximum(tops[0], tops[1]), bests[h])
+            if u == 0:
+                own_weight = jnp.exp2((self_scores[h] - best) * LOG2_SCALE)
+                total = own_weight
+                numer = own_weight.astype(jnp.bfloat16).astype(jnp.float32) * own_value
+            else:
+                shrink = jnp.exp2((bests[h] - best) * LOG2_SCALE)
+                total = totals[h] * shrink
+                numer = numers[h] * shrink
+            for j in range(2):
+                scale = jnp.exp2((tops[j] - best) * LOG2_SCALE)
+                total = total + scale * stats[:, j * 8 + HEADS + h : j * 8 + HEADS + h + 1]
+                numer = numer + scale * orecv[2 * u + j, h].astype(jnp.float32)
+            bests[h], totals[h], numers[h] = best, total, numer
     for h in range(HEADS):
-        tops = [stats[:, i * 8 + h : i * 8 + h + 1] for i in range(4)]
-        best = self_scores[h]
-        for one in tops:
-            best = jnp.maximum(best, one)
-        own_weight = jnp.exp2((self_scores[h] - best) * LOG2_SCALE)
-        total = own_weight
-        numer = own_weight.astype(jnp.bfloat16).astype(jnp.float32) * own_value
-        for i in range(4):
-            scale = jnp.exp2((tops[i] - best) * LOG2_SCALE)
-            total = total + scale * stats[:, i * 8 + HEADS + h : i * 8 + HEADS + h + 1]
-            numer = numer + scale * orecv[i, h].astype(jnp.float32)
-        att[:, h * HD : (h + 1) * HD] = (numer / total).astype(jnp.bfloat16)
+        att[:, h * HD : (h + 1) * HD] = (numers[h] / totals[h]).astype(jnp.bfloat16)
 
     loads[2].wait()
 
@@ -658,7 +679,7 @@
             vmem((2, 2, HEADS, ROWS, HD), bf16),
             vmem((2, 2, 8, ROWS), f32),
             vmem((4, HEADS, ROWS, HD), bf16),
-            vmem((128, ROWS), f32),
+            vmem((2, 128, ROWS), f32),
             vmem((8, ROWS), f32),
             vmem((3, 8, ROWS), f32),
             vmem((8, ROWS), f32),

time: 114 us -> 113 us (level)
  no operation moved by 1% of the time
where the time goes in v7:
time: 113 us
  Pallas kernels  110 us (97%)
  local copies, waits for them, and re-layouts  2.94 us (3%)
    pallas_call x1, Pallas kernels, per_device(): pl.pallas_call(body, out_shape=jax.ShapeDtypeStruct((16, 6144), bf16), in...  110 us

profile of v7, /device:TPU:0, one launch (start us, length us, event | category | flops | bytes accessed | tf_op | source)
XLA Modules:
  0.0 112.7 jit_solution(13085449971043158277)
XLA Ops:
  0.0 1.3 %reshape.6.gain = bf16[1,6144]{1,0:T(2,128)(2,1)} reshape(bf16[6144]{0:T(1024)(128)(2,1)} %param.11) | data formatting | bytes 24576 | tf_op jit(solution)/shard_map/reshape | solution.py:735
  1.3 109.7 %shard_map.100 = bf16[16,6144]{1,0:T(8,128)(2,1)} custom-call(bf16[256,384]{1,0:T(8,128)(2,1)} %hidden.1, bf16[1,6144]{1,0:T(2,128)(2,1)} %reshape.6.gain, bf16[6144,384]{1,0:T(8,128)(2,1)} %w_query.1, bf16[6144,128]{1,0:T(8,128)(2,1)} %w_keyval.1, bf16[384,6144]{1,0:T(8,128)(2,1)} %w_out.1, bf16[8,128,1024]{2,1,0:T(8,128)(2,1)} %key_pool.1, ...), custom_call_target="tpu_custom_call" | custom-call | flops 10000000000 | bytes 20000000 | tf_op jit(solution)/shard_map/pallas_call | solution.py:660
  111.0 1.6 %copy.12 = bf16[16,6144]{1,0:T(8,128)(2,1)} copy(bf16[16,6144]{1,0:T(8,128)(2,1)} %shard_map.100) | data formatting | bytes 393216

commit v8 on v7

--- a/solution.py
+++ b/solution.py
@@ -259,6 +259,7 @@
         if d == 1:
             forward(x_peer(d), half, half, 1, x_peer(3))
             forward(y_peer(d), 0, half, 0, y_peer(3))
+    lax.fori_loop(4, CHUNKS, send_stage, 0)
     shard = x_peer(2)
     arrived(shard, 0, half, 0)
     forward(shard, 0, half, 0, y_peer(1))
@@ -280,7 +281,6 @@
 
     pl.semaphore_wait(plane_sem, 2)
 
-    lax.fori_loop(4, 6, send_stage, 0)
     for d in range(3):
         landed(squares_y.at[d], sq_recv.at[1, d])
         square_sums = square_sums + squares_y[d]
@@ -332,13 +332,12 @@
         here = pltpu.make_async_copy(qown, dst, q_recv.at[u, own_half])
         return t == tp, here, there
 
-    for u in range(2):
+    for u in (1, 0):
         for j in range(2):
             same, here, there = q_copies(u, j)
             pl.when(same)(here.start)
             pl.when(jnp.logical_not(same))(there.start)
     own_copy.start()
-    lax.fori_loop(6, CHUNKS, send_stage, 0)
     lane = lax.broadcasted_iota(jnp.int32, (ROWS, HD), 1)
     first_request = seq // 2 * 8
     requests = jnp.broadcast_to(row_req[...], (HD, ROWS)).T

time: 113 us -> 113 us (level)
  no operation moved by 1% of the time
where the time goes in v8:
time: 113 us; the launch traced here: 112 us
  Pallas kernels  109 us (96%)
  local copies, waits for them, and re-layouts  2.94 us (3%)
    pallas_call x1, Pallas kernels, per_device(): pl.pallas_call(body, out_shape=jax.ShapeDtypeStruct((16, 6144), bf16), in...  109 us

profile of v8, /device:TPU:0, one launch (start us, length us, event | category | flops | bytes accessed | tf_op | source)
XLA Modules:
  0.0 112.4 jit_solution(9046606616417392700)
XLA Ops:
  0.0 1.3 %reshape.6.gain = bf16[1,6144]{1,0:T(2,128)(2,1)} reshape(bf16[6144]{0:T(1024)(128)(2,1)} %param.11) | data formatting | bytes 24576 | tf_op jit(solution)/shard_map/reshape | solution.py:734
  1.3 109.4 %shard_map.100 = bf16[16,6144]{1,0:T(8,128)(2,1)} custom-call(bf16[256,384]{1,0:T(8,128)(2,1)} %hidden.1, bf16[1,6144]{1,0:T(2,128)(2,1)} %reshape.6.gain, bf16[6144,384]{1,0:T(8,128)(2,1)} %w_query.1, bf16[6144,128]{1,0:T(8,128)(2,1)} %w_keyval.1, bf16[384,6144]{1,0:T(8,128)(2,1)} %w_out.1, bf16[8,128,1024]{2,1,0:T(8,128)(2,1)} %key_pool.1, ...), custom_call_target="tpu_custom_call" | custom-call | flops 10000000000 | bytes 20000000 | tf_op jit(solution)/shard_map/pallas_call | solution.py:659
  110.8 1.6 %copy.12 = bf16[16,6144]{1,0:T(8,128)(2,1)} copy(bf16[16,6144]{1,0:T(8,128)(2,1)} %shard_map.100) | data formatting | bytes 393216

commit v9 on v8

--- a/solution.py
+++ b/solution.py
@@ -18,8 +18,8 @@
 CHUNK = 8
 CHUNKS = 8
 STAGED = 6
-TILE = 512
-TILES = 6
+TILE = 1024
+TILES = 3
 MASKED = -1e30
 LOG2_SCALE = 1.4426950408889634 / HD**0.5
 

time: 113 us -> 113 us (level)
  no operation moved by 1% of the time
where the time goes in v9:
time: 113 us
  Pallas kernels  110 us (97%)
  local copies, waits for them, and re-layouts  2.94 us (3%)
    pallas_call x1, Pallas kernels, per_device(): pl.pallas_call(body, out_shape=jax.ShapeDtypeStruct((16, 6144), bf16), in...  110 us

profile of v9, /device:TPU:0, one launch (start us, length us, event | category | flops | bytes accessed | tf_op | source)
XLA Modules:
  0.0 112.5 jit_solution(576307382720281984)
XLA Ops:
  0.0 1.3 %reshape.6.gain = bf16[1,6144]{1,0:T(2,128)(2,1)} reshape(bf16[6144]{0:T(1024)(128)(2,1)} %param.11) | data formatting | bytes 24576 | tf_op jit(solution)/shard_map/reshape | solution.py:734
  1.3 109.6 %shard_map.100 = bf16[16,6144]{1,0:T(8,128)(2,1)} custom-call(bf16[256,384]{1,0:T(8,128)(2,1)} %hidden.1, bf16[1,6144]{1,0:T(2,128)(2,1)} %reshape.6.gain, bf16[6144,384]{1,0:T(8,128)(2,1)} %w_query.1, bf16[6144,128]{1,0:T(8,128)(2,1)} %w_keyval.1, bf16[384,6144]{1,0:T(8,128)(2,1)} %w_out.1, bf16[8,128,1024]{2,1,0:T(8,128)(2,1)} %key_pool.1, ...), custom_call_target="tpu_custom_call" | custom-call | flops 10000000000 | bytes 20000000 | tf_op jit(solution)/shard_map/pallas_call | solution.py:659
  110.9 1.6 %copy.12 = bf16[16,6144]{1,0:T(8,128)(2,1)} copy(bf16[16,6144]{1,0:T(8,128)(2,1)} %shard_map.100) | data formatting | bytes 393216
